TPU v7x, 128 devices: a whole 4x4x4 slice. The times are simulated.
128 devices in a mesh: row: 8 (over x, y_hi), col: 16 (over y_lo, z, core).
Axes of the slice: x: 4, y: 4 (y_hi: 2, y_lo: 2; y = y_hi * 2 + y_lo), z: 4, core: 2. Of those that a mesh axis runs over, the one named last changes fastest.
Arguments:
- amplitudes: float32 [8192, 8192], P('row', 'col'), may hold values from -6 to 6
- integrals: float32 [8192, 8192], P('row', 'col'), may hold values from -12 to 12
- factors: float32 [8192, 1024], P('col'), may hold values from -0.0625 to 0.0625
- pair_order: int32 [8192], replicated, may hold values from 0 to 8191, each once
- occ_energy: float32 [64], replicated, may hold values from -3 to -0.5
- vir_energy: float32 [128], replicated, may hold values from 0.5 to 4
Outputs:
- updated: float32 [8192, 8192], P('row', 'col')
Inputs may be any that keep to these rules, and one draw needn't show every extreme that they name: `pair_order`: every pair code appears exactly once.
All inputs are finite; a program needn't handle non-finite values.
Results may differ from a plain program's by a relative error of at most 0.0001.
Values sent between devices are 32-bit elements; how exact they have to be, the bound alone decides.
A program may use at most 64 MiB of HBM per device.

v0:
```python
import jax
import jax.numpy as jnp
from jax import lax
from jax.sharding import PartitionSpec as P

NO = 64
NV = 128
ITERS = 2


OMEGA = 0.6


def cut_along(value, dim, count):
    shape = value.shape
    blocks = value.reshape(*shape[:dim], count, shape[dim] // count, *shape[dim + 1 :])
    return jnp.moveaxis(blocks, dim, 0)


def sent_and_summed(value, axis, dim):
    count = lax.axis_size(axis)
    blocks = lax.all_to_all(cut_along(value, dim, count), axis, 0, 0, tiled=True)
    return jnp.sum(blocks, axis=0)


def pair_energy(pair_order, occ_energy, vir_energy):
    occupied = pair_order // NV
    virtual = pair_order % NV
    occ_hot = (occupied[:, None] == jnp.arange(NO, dtype=jnp.int32)[None, :]).astype(jnp.float32)
    vir_hot = (virtual[:, None] == jnp.arange(NV, dtype=jnp.int32)[None, :]).astype(jnp.float32)
    high = lax.Precision.HIGHEST
    return jnp.dot(vir_hot, vir_energy, precision=high) - jnp.dot(
        occ_hot, occ_energy, precision=high
    )


def contract(left, right):
    return lax.dot_general(left, right, (((1,), (1,)), ((), ())), precision=lax.Precision.HIGHEST)


def on_device(amplitudes, integrals, factors, pair_order, occ_energy, vir_energy):
    rows_tile, cols_tile = amplitudes.shape
    n_col = lax.axis_size("col")
    flat_rows = rows_tile // n_col
    row_id = lax.axis_index("row")
    col_id = lax.axis_index("col")
    energy = pair_energy(pair_order, occ_energy, vir_energy)
    row_energy = lax.dynamic_slice_in_dim(energy, row_id * rows_tile, rows_tile, 0)
    col_energy = lax.dynamic_slice_in_dim(energy, col_id * cols_tile, cols_tile, 0)
    amp = amplitudes
    for step in range(ITERS):

        def term(start, count, source=amp):
            return jnp.dot(source, factors, precision=lax.Precision.HIGHEST)

        shares = sent_and_summed(term(jnp.int32(0), flat_rows * lax.axis_size("col")), "col", 0)
        resid = integrals + contract(lax.all_gather(shares, "col", axis=0, tiled=True), factors)
        flat = lax.all_to_all(resid, "col", split_axis=0, concat_axis=1, tiled=True)
        mirrored = lax.all_to_all(flat, ("row", "col"), split_axis=1, concat_axis=0, tiled=True).T
        back = lax.all_to_all(mirrored, "col", split_axis=1, concat_axis=0, tiled=True)
        denom = row_energy[:, None] + col_energy[None, :]
        amp = (1.0 - OMEGA) * amp - OMEGA * (resid + back) / denom
    return amp


def solution(mesh):
    return jax.shard_map(
        on_device,
        mesh=mesh,
        in_specs=(P("row", "col"), P("row", "col"), P("col", None), P(), P(), P()),
        out_specs=P("row", "col"),
        check_vma=False,
    )
```

profile of v0, /device:TPU:1, one launch (start us, length us, event | category | flops | bytes accessed | tf_op | source)
XLA Modules:
  0.0 525.4 jit_solution(13291436998191489922)
XLA Ops:
  6.5 0.0 all-gather.3.cloned.1.call-start
  6.5 1.6 copy-done
  8.1 8.7 %fusion.12 = f32[1024,1024]{1,0:T(8,128)S(1)} fusion(f32[1024,512]{1,0:T(8,128)} %param.6, f32[512,1024]{1,0:T(8,128)S(1)} %copy-done), kind=kOutput, calls=%fused_computation.30 | convolution fusion | flops 6442450944 | bytes 8388608 | tf_op jit(solution)/shard_map/dot_general | solution.py:54
  16.9 56.9 %all_to_all.118 = f32[16,64,1024]{2,1,0:T(8,128)} all-to-all(f32[16,64,1024]{2,1,0:T(8,128)S(1)} %bitcast.68), channel_id=1, replica_groups=mesh['row'=8,'col'=16] {'col'}, dimensions={0} | all-to-all | bytes 8388608 | tf_op jit(solution)/shard_map/all_to_all | solution.py:22
  73.7 3.2 reduce_sum.18
  76.9 0.0 all-gather.3.cloned.1.call-update
  76.9 37.5 %all-gather.3.cloned.1.call-done = f32[1024,1024]{1,0:T(8,128)} async-done(((f32[64,1024]{1,0:T(8,128)}), f32[1024,1024]{1,0:T(8,128)}) %all-gather.3.cloned.1.call-update) | async-done | bytes 4194320 | tf_op jit(solution)/shard_map/all_gather | solution.py:57
  114.5 9.0 %convolution_add_fusion.1 = f32[1024,512]{1,0:T(8,128)S(1)} fusion(f32[1024,512]{1,0:T(8,128)} %param.7, f32[1024,1024]{1,0:T(8,128)} %all-gather.3.cloned.1.call-done, f32[512,1024]{1,0:T(8,128)S(1)} %copy-done), kind=kOutput, calls=%fused_computation.16 | convolution fusion | flops 6442975232 | bytes 10485760 | tf_op jit(solution)/shard_map/dot_general | solution.py:38
  123.4 0.0 copy-start.1
  123.4 31.4 %all_to_all.119 = f32[16,64,512]{2,1,0:T(8,128)S(1)} all-to-all(f32[16,64,512]{2,1,0:T(8,128)S(1)} %bitcast.62), channel_id=1, replica_groups=mesh['row'=8,'col'=16] {'col'}, dimensions={0} | all-to-all | bytes 4194304 | tf_op jit(solution)/shard_map/all_to_all | solution.py:58
  154.9 2.5 copy.21
  157.4 4.4 all_to_all.90
  161.8 6.6 %copy.40 = f32[64,128,64]{2,0,1:T(8,128)} copy(f32[64,128,64]{2,1,0:T(8,128)} %all_to_all.90) | data formatting | bytes 4194304 | tf_op jit(solution)/shard_map/all_to_all | solution.py:59
  168.4 5.5 %reshape.36 = f32[128,1,4096]{2,1,0:T(1,128)} reshape(f32[128,64,64]{2,1,0:T(8,128)} %bitcast.66) | data formatting | bytes 4194304
  173.9 38.4 %all_to_all.120 = f32[128,1,4096]{2,1,0:T(1,128)} all-to-all(f32[128,1,4096]{2,1,0:T(1,128)} %reshape.36), channel_id=1, replica_groups=mesh['row'=8,'col'=16] {'row','col'}, dimensions={0} | all-to-all | bytes 4194304 | tf_op jit(solution)/shard_map/all_to_all | solution.py:59
  212.3 0.5 broadcast.30
  212.8 8.5 %reduce = f32[128,4096]{1,0:T(8,128)} reduce(f32[128,1,4096]{2,1,0:T(1,128)} %all_to_all.120, f32[]{:T(128)} %broadcast.30), dimensions={1}, to_apply=%all_to_all.91.reduce_sub_computation | reduce | bytes 4194308 | tf_op jit(solution)/shard_map/all_to_all | solution.py:59
  221.3 4.6 reshape.37
  226.0 3.8 copy.29
  229.7 3.2 copy.38
  232.9 5.5 %all-to-all-start.3 = ((f32[64,16,512]{2,0,1:T(8,128)}), f32[64,16,512]{2,0,1:T(8,128)}, u32[]{:S(2)}, u32[]{:S(2)}) async-start(f32[64,16,512]{2,0,1:T(8,128)} %bitcast.72), calls=%async_computation.3 | async-start | bytes 4194304 | tf_op jit(solution)/shard_map/all_to_all | solution.py:60
  238.4 0.2 all-gather.5.cloned.1.call-start
  238.7 0.0 copy-done.6
  238.7 0.7 fusion.6
  239.5 2.9 fusion
  242.4 0.1 dynamic_slice.7
  242.5 24.1 %all-to-all-done.3 = f32[64,16,512]{2,0,1:T(8,128)} async-done(((f32[64,16,512]{2,0,1:T(8,128)}), f32[64,16,512]{2,0,1:T(8,128)}, u32[]{:S(2)}, u32[]{:S(2)}) %all-to-all-start.3) | async-done | bytes 2097184 | tf_op jit(solution)/shard_map/all_to_all | solution.py:60
  266.6 3.4 fusion.1
  270.1 7.2 %fusion.13 = f32[1024,1024]{1,0:T(8,128)S(1)} fusion(f32[1024,512]{1,0:T(8,128)S(1)} %fusion.1, f32[512,1024]{1,0:T(8,128)S(1)} %copy-done), kind=kOutput, calls=%fused_computation.31 | convolution fusion | flops 6442450944 | bytes 8388608 | tf_op jit(solution)/shard_map/dot_general | solution.py:54
  277.2 55.2 %all_to_all.121 = f32[16,64,1024]{2,1,0:T(8,128)} all-to-all(f32[16,64,1024]{2,1,0:T(8,128)S(1)} %bitcast.69), channel_id=1, replica_groups=mesh['row'=8,'col'=16] {'col'}, dimensions={0} | all-to-all | bytes 8388608 | tf_op jit(solution)/shard_map/all_to_all | solution.py:22
  332.5 3.2 reduce_sum.19
  335.6 0.0 all-gather.5.cloned.1.call-update
  335.7 33.7 %all-gather.5.cloned.1.call-done = f32[1024,1024]{1,0:T(8,128)} async-done(((f32[64,1024]{1,0:T(8,128)}), f32[1024,1024]{1,0:T(8,128)}) %all-gather.5.cloned.1.call-update) | async-done | bytes 4194320 | tf_op jit(solution)/shard_map/all_gather | solution.py:57
  369.4 9.0 %convolution_add_fusion = f32[1024,512]{1,0:T(8,128)S(1)} fusion(f32[1024,512]{1,0:T(8,128)} %param.7, f32[1024,1024]{1,0:T(8,128)} %all-gather.5.cloned.1.call-done, f32[512,1024]{1,0:T(8,128)S(1)} %copy-done), kind=kOutput, calls=%fused_computation.15 | convolution fusion | flops 6442975232 | bytes 10485760 | tf_op jit(solution)/shard_map/dot_general | solution.py:38
  378.3 0.0 copy-start.2
  378.4 30.9 %all_to_all.122 = f32[16,64,512]{2,1,0:T(8,128)S(1)} all-to-all(f32[16,64,512]{2,1,0:T(8,128)S(1)} %bitcast.63), channel_id=1, replica_groups=mesh['row'=8,'col'=16] {'col'}, dimensions={0} | all-to-all | bytes 4194304 | tf_op jit(solution)/shard_map/all_to_all | solution.py:58
  409.3 2.5 copy.25
  411.8 4.4 all_to_all.102
  416.2 6.6 %copy.39 = f32[64,128,64]{2,0,1:T(8,128)} copy(f32[64,128,64]{2,1,0:T(8,128)} %all_to_all.102) | data formatting | bytes 4194304 | tf_op jit(solution)/shard_map/all_to_all | solution.py:59
  422.8 5.5 %reshape.38 = f32[128,1,4096]{2,1,0:T(1,128)} reshape(f32[128,64,64]{2,1,0:T(8,128)} %bitcast.67) | data formatting | bytes 4194304
  428.3 38.5 %all_to_all.123 = f32[128,1,4096]{2,1,0:T(1,128)} all-to-all(f32[128,1,4096]{2,1,0:T(1,128)} %reshape.38), channel_id=1, replica_groups=mesh['row'=8,'col'=16] {'row','col'}, dimensions={0} | all-to-all | bytes 4194304 | tf_op jit(solution)/shard_map/all_to_all | solution.py:59
  466.8 8.5 %reduce.1 = f32[128,4096]{1,0:T(8,128)} reduce(f32[128,1,4096]{2,1,0:T(1,128)} %all_to_all.123, f32[]{:T(128)} %broadcast.30), dimensions={1}, to_apply=%all_to_all.103.reduce_sub_computation | reduce | bytes 4194308 | tf_op jit(solution)/shard_map/all_to_all | solution.py:59
  475.4 4.6 reshape.39
  480.0 3.8 copy.30
  483.8 1.8 copy.37
  485.6 0.0 copy-start.3
  485.6 30.6 %all_to_all.124 = f32[64,16,512]{2,0,1:T(8,128)S(1)} all-to-all(f32[64,16,512]{2,0,1:T(8,128)S(1)} %bitcast.73), channel_id=1, replica_groups=mesh['row'=8,'col'=16] {'col'}, dimensions={1} | all-to-all | bytes 4194304 | tf_op jit(solution)/shard_map/all_to_all | solution.py:60
  516.2 1.9 fusion.2
  (16 shorter events, 0.1 us)
Async XLA Ops:
  6.5 1.6 copy-start
  6.5 107.9 %all-gather.3.cloned.1.call-start = ((), (), s32[]{:S(2)}) async-start(), calls=%async_computation.8 | async-start | bytes 4456448 | tf_op jit(solution)/shard_map/all_gather | solution.py:57
  123.4 31.5 %copy-start.1 = (f32[1024,512]{1,0:T(8,128)}, f32[1024,512]{1,0:T(8,128)S(1)}, u32[]{:S(2)}) copy-start(f32[1024,512]{1,0:T(8,128)S(1)} %convolution_add_fusion.1) | copy-start | bytes 6291460
  232.9 5.7 %copy-start.6 = (s32[8192]{0:T(1024)S(1)}, s32[8192]{0:T(1024)}, u32[]{:S(2)}) copy-start(s32[8192]{0:T(1024)} %param.9) | copy-start | bytes 98308
  232.9 5.8 %copy-start.7 = (f32[64]{0:T(128)S(1)}, f32[64]{0:T(128)}, u32[]{:S(2)}) copy-start(f32[64]{0:T(128)} %param.10) | copy-start | bytes 772
  232.9 6.5 %copy-start.8 = (f32[128]{0:T(128)S(1)}, f32[128]{0:T(128)}, u32[]{:S(2)}) copy-start(f32[128]{0:T(128)} %param.11) | copy-start | bytes 1540
  232.9 33.7 %all-to-all-start.3 = ((f32[64,16,512]{2,0,1:T(8,128)}), f32[64,16,512]{2,0,1:T(8,128)}, u32[]{:S(2)}, u32[]{:S(2)}) async-start(f32[64,16,512]{2,0,1:T(8,128)} %bitcast.72), calls=%async_computation.3 | async-start | bytes 4194304 | tf_op jit(solution)/shard_map/all_to_all | solution.py:60
  238.4 131.0 %all-gather.5.cloned.1.call-start = ((), (), s32[]{:S(2)}) async-start(), calls=%async_computation.9 | async-start | bytes 4456448 | tf_op jit(solution)/shard_map/all_gather | solution.py:57
  270.0 7.2 %copy-start.4 = (f32[1024,512]{1,0:T(8,128)}, f32[1024,512]{1,0:T(8,128)S(1)}, u32[]{:S(2)}) copy-start(f32[1024,512]{1,0:T(8,128)S(1)} %fusion.1) | copy-start | bytes 6291460
  378.3 30.9 %copy-start.2 = (f32[1024,512]{1,0:T(8,128)}, f32[1024,512]{1,0:T(8,128)S(1)}, u32[]{:S(2)}) copy-start(f32[1024,512]{1,0:T(8,128)S(1)} %convolution_add_fusion) | copy-start | bytes 6291460
  485.6 30.6 %copy-start.3 = (f32[1024,512]{1,0:T(8,128)S(1)}, f32[1024,512]{1,0:T(8,128)}, u32[]{:S(2)}) copy-start(f32[1024,512]{1,0:T(8,128)} %copy-done.2) | copy-start | bytes 6291460
  485.6 30.6 %copy-start.5 = (f32[1024,512]{1,0:T(8,128)S(1)}, f32[1024,512]{1,0:T(8,128)}, u32[]{:S(2)}) copy-start(f32[1024,512]{1,0:T(8,128)} %copy-done.4) | copy-start | bytes 6291460
Sparse Core Ops, SparseCore 0:
  77.1 37.3 all-gather.2
  335.8 33.5 all-gather.4
where the time goes:
time: 534 us; the launch traced here: 525 us
  blocking collectives  282 us (53%)
  waiting for transfers between devices  95.4 us (18%)
  local copies, waits for them, and re-layouts  62 us (12%)
  matrix products  37.5 us (7%)
  other arithmetic  28.8 us (5%)
  between operations  14.1 us (3%)
  starting transfers between devices  5.71 us (1%)
    all_to_all x2, blocking collectives, sent_and_summed(): lax.all_to_all(cut_along(value, dim, count), axis, 0, 0, tiled=True)  112 us
    all_to_all x2, blocking collectives, on_device(): lax.all_to_all(flat, ('row', 'col'), split_axis=1, concat_axis=0, tiled=T...  76.9 us
    all_gather x2, waiting for transfers between devices, on_device(): lax.all_gather(shares, 'col', axis=0, tiled=True)  71.2 us
    all_to_all x2, blocking collectives, on_device(): flat = lax.all_to_all(resid, 'col', split_axis=0, concat_axis=1, tiled=True)  62.4 us
    all_to_all x1, blocking collectives, on_device(): lax.all_to_all(mirrored, 'col', split_axis=1, concat_axis=0, tiled=True)  30.6 us
    all_to_all x7, local copies, waits for them, and re-layouts, on_device(): lax.all_to_all(flat, ('row', 'col'), split_axis=1, concat_axis=0, tiled=T...  30 us
    all_to_all x1, waiting for transfers between devices, on_device(): lax.all_to_all(mirrored, 'col', split_axis=1, concat_axis=0, tiled=True)  24.1 us
    unnamed x22, local copies, waits for them, and re-layouts  21.9 us
  transfers between devices with their start and end apart: 3, of which 3 were waited for; matrix products, arithmetic and copies ran while one was open for 1% of the time, Pallas kernels for 0%

commit v1 on v0

v1 whole, which is shorter than its diff:
```python
import jax
import jax.numpy as jnp
from jax import lax
from jax.experimental import pallas as pl
from jax.experimental.pallas import tpu as pltpu
from jax.sharding import PartitionSpec as P

NO = 64
NV = 128
OMEGA = 0.6
KEEP = 1.0 - OMEGA

MESH = pl.DeviceIdType.MESH
F32 = jnp.float32
BF16 = jnp.bfloat16
N_SEM = 160


def pair_energy(pair_order, occ_energy, vir_energy):
    occ_hit = (pair_order // NV)[:, None] == jnp.arange(NO, dtype=jnp.int32)[None, :]
    vir_hit = (pair_order % NV)[:, None] == jnp.arange(NV, dtype=jnp.int32)[None, :]
    return jnp.sum(jnp.where(vir_hit, vir_energy[None, :], 0.0), axis=1) - jnp.sum(
        jnp.where(occ_hit, occ_energy[None, :], 0.0), axis=1
    )


def rem(a, b):
    return lax.rem(a, jnp.int32(b))


def div(a, b):
    return lax.div(a, jnp.int32(b))


def split(value):
    high = value.astype(BF16)
    return high, (value - high.astype(F32)).astype(BF16)


def dot_nn(a, b):
    return lax.dot_general(a, b, (((1,), (0,)), ((), ())), preferred_element_type=F32)


def dot_nt(a, b):
    return lax.dot_general(a, b, (((1,), (1,)), ((), ())), preferred_element_type=F32)


def triple(dot, ah, al, bh, bl):
    return dot(ah, bh) + (dot(ah, bl) + dot(al, bh))


class Axis:
    def __init__(self, me, ring, mate, index, device, pick):
        self.me, self.ring, self.mate = me, ring, mate
        self.index, self.device, self.pick = index, device, pick


def kernel(
    a_ref, v_ref, f_ref, er_ref, ec_ref, o_ref,
    a_in, v_in, f_sib, fk_hl, fr, fr_hl, pa, pb, land_c, land_r, mate_c, mate_r,
    sum_c, sum_r, own_c, own_r, inter, y_out, y_in, lh, lf, lt, wr, wk,
    b1, b2, b3, vt_sib, t1, t2, u1, u2, uf, ss, rs, ls,
):
    row = lax.axis_index("row")
    q = lax.axis_index("col")
    c = rem(q, 2)
    o = 1 - c
    k = div(q, 8) * 4 + rem(div(q, 2), 4)
    col_ax = Axis(
        k, rem(div(q, 2), 4), div(q, 8),
        lambda ring, mate: mate * 4 + ring,
        lambda i: (row, div(i, 4) * 8 + rem(i, 4) * 2 + c),
        lambda ref, i: ref.at[i],
    )
    row_ax = Axis(
        row, div(row, 2), rem(row, 2),
        lambda ring, mate: ring * 2 + mate,
        lambda i: (i, q),
        lambda ref, i: ref.at[:, i],
    )
    sibling = (row, q + 1 - 2 * c)

    barrier = pltpu.get_barrier_semaphore()
    for ax in (col_ax, row_ax):
        for d in range(1, 8):
            pl.semaphore_signal(barrier, inc=1, device_id=ax.device(rem(ax.me + d, 8)), device_id_type=MESH)
    pl.semaphore_signal(barrier, inc=1, device_id=sibling, device_id_type=MESH)
    pl.semaphore_wait(barrier, 15)

    used = [0, 0]
    pending = {}

    def send(src, dst, device):
        i = used[0]
        used[0] += 1
        copy = pltpu.make_async_remote_copy(
            src_ref=src, dst_ref=dst, send_sem=ss.at[i], recv_sem=rs.at[i],
            device_id=device, device_id_type=MESH,
        )
        copy.start()
        pending[id(copy)] = copy
        return copy

    def local(src, dst):
        i = used[1]
        used[1] += 1
        copy = pltpu.make_async_copy(src, dst, ls.at[i])
        copy.start()
        return copy

    def sent(copies):
        for copy in copies:
            if pending.pop(id(copy), None) is not None:
                copy.wait_send()

    def all_to_all(ax, src, dst):
        mine = local(src(ax.me), dst(ax.me))
        copies = []
        for d in (4, 3, 5, 2, 6, 1, 7):
            to = rem(ax.me + d, 8)
            copies.append(send(src(to), dst(ax.me), ax.device(to)))

        def wait():
            for copy in copies:
                copy.wait_recv()
            mine.wait()

        return wait

    def scatter_start(ax, part, land):
        copies = []
        for m in range(2):
            mate = (1 - ax.mate) if m == 0 else ax.mate
            for d in (2, 1, 3):
                ring = rem(ax.ring + d, 4)
                copies.append(
                    send(
                        ax.pick(part, ax.index(ring, mate)),
                        land.at[d - 1, m],
                        ax.device(ax.index(ring, ax.mate)),
                    )
                )
        return copies

    def scatter_mate(ax, part, land, copies, stage, mate_land):
        for copy in copies[:3]:
            copy.wait_recv()
        stage[...] = (ax.pick(part, ax.index(ax.ring, 1 - ax.mate))[...] + land[0, 0]) + (land[1, 0] + land[2, 0])
        return send(stage, mate_land, ax.device(ax.index(ax.ring, 1 - ax.mate)))

    def scatter_end(ax, part, land, copies, mate_copy, mate_land):
        for copy in copies[3:]:
            copy.wait_recv()
        value = (ax.pick(part, ax.me)[...] + land[0, 1]) + (land[1, 1] + land[2, 1])
        mate_copy.wait_recv()
        return value + mate_land[...]

    def gather_start(ax, full):
        piece = ax.pick(full, ax.me)
        mate = send(piece, piece, ax.device(ax.index(ax.ring, 1 - ax.mate)))
        copies = []
        for d in (2, 1, 3):
            copies.append(send(piece, piece, ax.device(ax.index(rem(ax.ring + d, 4), ax.mate))))
        return mate, copies

    def gather_forward(ax, full, started):
        mate, copies = started
        mate.wait_recv()
        piece = ax.pick(full, ax.index(ax.ring, 1 - ax.mate))
        for d in (2, 1, 3):
            copies.append(send(piece, piece, ax.device(ax.index(rem(ax.ring + d, 4), ax.mate))))

    def gather_end(started):
        for copy in started[1]:
            copy.wait_recv()

    def lanes(n, size):
        return pl.ds(pl.multiple_of(n * size, size), size)

    a_copy = send(a_ref.at[o], a_in, sibling)
    f_copy = send(f_ref, f_sib, sibling)
    f_hop1 = all_to_all(col_ax, lambda i: f_ref.at[i, row], lambda i: uf.at[i])
    v_copy = send(v_ref.at[o], v_in, sibling)
    v_hop1 = all_to_all(row_ax, lambda i: v_ref.at[:, i], lambda i: b1.at[i])

    fk_hl[0, c], fk_hl[1, c] = split(f_ref[...].reshape(512, 1024))
    lh[0, :, lanes(c, 512)], lh[1, :, lanes(c, 512)] = split(a_ref[c])
    a_copy.wait_recv()
    lh[0, :, lanes(o, 512)], lh[1, :, lanes(o, 512)] = split(a_in[...])
    f_copy.wait_recv()
    fk_hl[0, o], fk_hl[1, o] = split(f_sib[...].reshape(512, 1024))
    f_hop1()
    f_hop2 = all_to_all(row_ax, lambda i: uf.at[i], lambda i: fr.at[c, k, i])

    def product_nn(left, right, out):
        @pl.loop(0, 4)
        def _(n):
            cols = lanes(n, 256)
            res = triple(
                dot_nn, left[0], left[1],
                right[0, :, :, cols].reshape(1024, 256), right[1, :, :, cols].reshape(1024, 256),
            )
            out[:, :, :, cols] = res.reshape(8, 8, 8, 256)

    product_nn(lh, fk_hl, pa)
    rs0 = scatter_start(col_ax, pa, land_c)
    f_hop2()
    f_gather = gather_start(col_ax, fr.at[c])
    mate0 = scatter_mate(col_ax, pa, land_c, rs0, sum_c, mate_c)
    i_own = scatter_end(col_ax, pa, land_c, rs0, mate0, mate_c)
    inter[k] = i_own
    i_gather = gather_start(col_ax, inter)
    gather_forward(col_ax, inter, i_gather)
    gather_forward(col_ax, fr.at[c], f_gather)
    v_hop1()
    v_hop2 = all_to_all(col_ax, lambda i: b1.at[i], lambda i: b2.at[i])
    gather_end(i_gather)

    lf[0], lf[1] = split(inter[...].reshape(512, 1024))
    v_copy.wait_recv()

    @pl.loop(0, 2)
    def _(n):
        rows = lanes(n, 256)
        res = triple(dot_nt, lf[0], lf[1], fk_hl[0, o, rows], fk_hl[1, o, rows])
        drive = v_in[:, :, rows].reshape(512, 256)
        y = (drive + res) / (er_ref[c] + ec_ref[o, :, rows])
        y_out[:, rows] = y
        at = pl.ds(pl.multiple_of(o * 512 + n * 256, 256), 256)
        lh[0, :, at], lh[1, :, at] = split(y)

    y_copy = send(y_out, y_in, sibling)

    @pl.loop(0, 2)
    def _(n):
        rows = lanes(n, 256)
        res = triple(dot_nt, lf[0], lf[1], fk_hl[0, c, rows], fk_hl[1, c, rows])
        drive = v_ref[c, :, :, rows].reshape(512, 256)
        y = (drive + res) / (er_ref[c] + ec_ref[c, :, rows])
        at = pl.ds(pl.multiple_of(c * 512 + n * 256, 256), 256)
        lh[0, :, at], lh[1, :, at] = split(y)
        lt[0, rows, lanes(c, 512)], lt[1, rows, lanes(c, 512)] = split(y.T)

    sent(rs0)
    product_nn(lh, fk_hl, pa)
    rs1_c = scatter_start(col_ax, pa, land_c)
    gather_end(f_gather)
    f_copy2 = send(fr.at[c], fr.at[c], sibling)
    fr_hl[0, c], fr_hl[1, c] = split(fr[c].reshape(512, 1024))
    y_copy.wait_recv()

    @pl.loop(0, 2)
    def _(n):
        rows = lanes(n, 256)
        lt[0, rows, lanes(o, 512)], lt[1, rows, lanes(o, 512)] = split(y_in[:, rows].T)

    f_copy2.wait_recv()
    fr_hl[0, o], fr_hl[1, o] = split(fr[o].reshape(512, 1024))
    product_nn(lt, fr_hl, pb)
    rs1_r = scatter_start(row_ax, pb, land_r)
    v_hop2()
    v_hop3 = all_to_all(row_ax, lambda i: b2.at[i], lambda i: b3.at[i])

    sent([mate0])
    mate1_c = scatter_mate(col_ax, pa, land_c, rs1_c, sum_c, mate_c)
    mate1_r = scatter_mate(row_ax, pb, land_r, rs1_r, sum_r, mate_r)
    own_c[...] = (2.0 * KEEP * OMEGA) * i_own - (OMEGA * OMEGA) * scatter_end(
        col_ax, pa, land_c, rs1_c, mate1_c, mate_c
    )
    c_hop1 = all_to_all(row_ax, lambda i: own_c.at[i], lambda i: t1.at[i])
    own_r[...] = -(OMEGA * OMEGA) * scatter_end(row_ax, pb, land_r, rs1_r, mate1_r, mate_r)
    r_hop1 = all_to_all(col_ax, lambda i: own_r.at[i], lambda i: u1.at[i])
    c_hop1()
    c_hop2 = all_to_all(col_ax, lambda i: t1.at[i], lambda i: t2.at[i])
    r_hop1()
    r_hop2 = all_to_all(row_ax, lambda i: u1.at[i], lambda i: u2.at[i])
    c_hop2()
    row_ax.pick(wk, row)[...] = own_r[...] + t2[...]
    k_gather = gather_start(row_ax, wk)
    r_hop2()
    wr[c, k] = own_c[...] + u2[...]
    r_gather = gather_start(col_ax, wr.at[c])
    gather_forward(row_ax, wk, k_gather)
    gather_forward(col_ax, wr.at[c], r_gather)
    v_hop3()
    vt_copy = send(b3.at[:, o], vt_sib, sibling)
    gather_end(r_gather)
    w_copy = send(wr.at[c], wr.at[c], sibling)
    lf[0], lf[1] = split(wr[c].reshape(512, 1024))
    gather_end(k_gather)
    lt[0], lt[1] = split(wk[...].reshape(512, 1024))

    def finish(half, mirrored):
        @pl.loop(0, 2)
        def _(n):
            rows = lanes(n, 256)
            res = triple(dot_nt, lf[0], lf[1], fk_hl[0, c, rows], fk_hl[1, c, rows])
            res = res + triple(dot_nt, fr_hl[0, half], fr_hl[1, half], lt[0, rows], lt[1, rows])
            drive = v_ref[half, :, :, rows].reshape(512, 256) + mirrored(n).reshape(256, 512).T
            sym = (1.0 + KEEP) * OMEGA * drive + res
            o_ref[half, :, rows] = (KEEP * KEEP) * a_ref[half, :, rows] - sym / (
                er_ref[half] + ec_ref[c, :, rows]
            )

    finish(c, lambda n: b3[pl.ds(n * 4, 4), c])
    w_copy.wait_recv()
    lf[0], lf[1] = split(wr[o].reshape(512, 1024))
    vt_copy.wait_recv()
    finish(o, lambda n: vt_sib[pl.ds(n * 4, 4)])
    sent(list(pending.values()))


def on_device(amplitudes, integrals, factors, pair_order, occ_energy, vir_energy):
    row = lax.axis_index("row")
    q = lax.axis_index("col")
    order = jnp.concatenate(
        [
            lax.dynamic_slice_in_dim(pair_order, row * 1024, 1024, 0),
            lax.dynamic_slice_in_dim(pair_order, (q // 2) * 1024, 1024, 0),
        ]
    )
    energy = pair_energy(order, occ_energy, vir_energy)
    big = lambda *shape: pltpu.VMEM(shape, F32)
    half = lambda *shape: pltpu.VMEM(shape, BF16)
    out = pl.pallas_call(
        kernel,
        out_shape=jax.ShapeDtypeStruct((2, 512, 512), F32),
        in_specs=[pl.BlockSpec(memory_space=pltpu.VMEM)] * 5,
        out_specs=pl.BlockSpec(memory_space=pltpu.VMEM),
        scratch_shapes=[
            big(512, 512),
            big(8, 64, 512),
            big(8, 8, 8, 1024),
            half(2, 2, 512, 1024),
            big(2, 8, 8, 8, 1024),
            half(2, 2, 512, 1024),
            big(8, 8, 8, 1024),
            big(8, 8, 8, 1024),
            big(3, 2, 8, 8, 1024),
            big(3, 2, 8, 8, 1024),
            big(8, 8, 1024),
            big(8, 8, 1024),
            big(8, 8, 1024),
            big(8, 8, 1024),
            big(8, 8, 1024),
            big(8, 8, 1024),
            big(8, 8, 8, 1024),
            big(512, 512),
            big(512, 512),
            half(2, 512, 1024),
            half(2, 512, 1024),
            half(2, 512, 1024),
            big(2, 8, 8, 8, 1024),
            big(8, 8, 8, 1024),
            big(8, 2, 64, 512),
            big(8, 2, 64, 512),
            big(8, 2, 64, 512),
            big(8, 64, 512),
            big(8, 8, 1024),
            big(8, 8, 1024),
            big(8, 8, 1024),
            big(8, 8, 1024),
            big(8, 8, 1024),
            pltpu.SemaphoreType.DMA((N_SEM,)),
            pltpu.SemaphoreType.DMA((N_SEM,)),
            pltpu.SemaphoreType.DMA((16,)),
        ],
        compiler_params=pltpu.CompilerParams(
            collective_id=0, has_side_effects=True, vmem_limit_bytes=63 * 2**20
        ),
        name="lambda_steps",
    )(
        amplitudes.reshape(2, 512, 512),
        integrals.reshape(2, 8, 64, 512),
        factors.reshape(8, 8, 8, 1024),
        energy[:1024].reshape(2, 512, 1),
        energy[1024:].reshape(2, 1, 512),
    )
    return out.reshape(1024, 512)


def solution(mesh):
    return jax.shard_map(
        on_device,
        mesh=mesh,
        in_specs=(P("row", "col"), P("row", "col"), P("col", None), P(), P(), P()),
        out_specs=P("row", "col"),
        check_vma=False,
    )
```

time: 534 us -> 221 us (0.41); the launches traced: 525 us -> 221 us
  blocking collectives: 282 us -> 0 us
  Pallas kernels: 0 us -> 213 us
  waiting for transfers between devices: 95.4 us -> 0 us
  local copies, waits for them, and re-layouts: 62 us -> 5.57 us
  matrix products: 37.5 us -> 0 us
  other arithmetic: 28.8 us -> 2.12 us
  between operations: 14.1 us -> 0.03 us
  starting transfers between devices: 5.71 us -> 0 us
    all_to_all x7 -> x0, blocking collectives: 282 us -> none  [the longest x2 112 us: sent_and_summed(): lax.all_to_all(cut_along(value, dim, count), axis, 0, 0, tiled=True)]
    pallas_call x0 -> x1, Pallas kernels: none -> 213 us  [on_device(): pl.pallas_call(kernel, out_shape=jax.ShapeDtypeStruct((2, 512, 512), F32)...]
    all_gather x2 -> x0, waiting for transfers between devices: 71.2 us -> none  [on_device(): lax.all_gather(shares, 'col', axis=0, tiled=True)]
    all_to_all x11 -> x0, local copies, waits for them, and re-layouts: 40.1 us -> none  [the longest x7 30 us: on_device(): lax.all_to_all(flat, ('row', 'col'), split_axis=1, concat_axis=0, tiled=T...]
    dot_general x6 -> x0, matrix products: 37.5 us -> none  [the longest x2 17.9 us: contract(): lax.dot_general(left, right, (((1,), (1,)), ((), ())), precision=lax.Prec...]
    all_to_all x1 -> x0, waiting for transfers between devices: 24.1 us -> none  [on_device(): lax.all_to_all(mirrored, 'col', split_axis=1, concat_axis=0, tiled=True)]
    unnamed x22 -> x1, local copies, waits for them, and re-layouts: 21.9 us -> 3.08 us
    all_to_all x2 -> x0, other arithmetic: 17.1 us -> none  [on_device(): lax.all_to_all(flat, ('row', 'col'), split_axis=1, concat_axis=0, tiled=T...]
  transfers between devices with their start and end apart: 3 -> 0, of which waited for: 3 -> 0; matrix products, arithmetic and copies ran while one was open for 1% -> 0% of each run, Pallas kernels for 0% -> 0%
where the time goes in v1:
time: 221 us
  Pallas kernels  213 us (96%)
  local copies, waits for them, and re-layouts  5.57 us (3%)
    pallas_call x1, Pallas kernels, on_device(): pl.pallas_call(kernel, out_shape=jax.ShapeDtypeStruct((2, 512, 512), F32)...  213 us

profile of v1, /device:TPU:1, one launch (start us, length us, event | category | flops | bytes accessed | tf_op | source)
XLA Modules:
  0.0 221.0 jit_solution(9765217243942548516)
XLA Ops:
  0.0 0.8 fusion.1
  0.8 0.8 select_reduce_fusion.1
  1.6 1.3 select_reduce_fusion
  2.9 0.6 fusion.2
  3.5 1.1 slice.18.er_ref
  4.6 213.3 %lambda_steps.1 = f32[2,512,512]{2,1,0:T(8,128)} custom-call(f32[2,512,512]{2,1,0:T(8,128)} %bitcast.6, f32[2,8,64,512]{3,2,1,0:T(8,128)} %bitcast.7, f32[8,8,8,1024]{3,2,1,0:T(8,128)} %bitcast.8, f32[2,512,1]{2,1,0:T(8,128)} %slice.18.er_ref, f32[2,1,512]{2,1,0:T(1,128)} %bitcast.9), custom_call_target="tpu_custom_call" | custom-call | tf_op jit(solution)/shard_map/lambda_steps/pallas_call | solution.py:325
  217.9 3.1 %copy.10 = f32[1024,512]{1,0:T(8,128)} copy(f32[1024,512]{1,0:T(8,128)} %bitcast.5) | data formatting | bytes 4194304
  (2 shorter events, 0.0 us)

commit v2 on v1

--- a/solution.py
+++ b/solution.py
@@ -50,14 +50,14 @@
 
 
 class Axis:
-    def __init__(self, me, ring, mate, index, device, pick):
+    def __init__(self, me, ring, mate, index, device, pick, half):
         self.me, self.ring, self.mate = me, ring, mate
-        self.index, self.device, self.pick = index, device, pick
+        self.index, self.device, self.pick, self.half = index, device, pick, half
 
 
 def kernel(
     a_ref, v_ref, f_ref, er_ref, ec_ref, o_ref,
-    a_in, v_in, f_sib, fk_hl, fr, fr_hl, pa, pb, land_c, land_r, mate_c, mate_r,
+    a_in, v_in, f_sib, fk_hl, fr, fr_hl, pa, pb, far_c, near_c, far_r, near_r, mate_c, mate_r,
     sum_c, sum_r, own_c, own_r, inter, y_out, y_in, lh, lf, lt, wr, wk,
     b1, b2, b3, vt_sib, t1, t2, u1, u2, uf, ss, rs, ls,
 ):
@@ -71,12 +71,14 @@
         lambda ring, mate: mate * 4 + ring,
         lambda i: (row, div(i, 4) * 8 + rem(i, 4) * 2 + c),
         lambda ref, i: ref.at[i],
+        lambda ref, i, h: ref.at[i, pl.ds(4 * h, 4)],
     )
     row_ax = Axis(
         row, div(row, 2), rem(row, 2),
         lambda ring, mate: ring * 2 + mate,
         lambda i: (i, q),
         lambda ref, i: ref.at[:, i],
+        lambda ref, i, h: ref.at[pl.ds(4 * h, 4), i],
     )
     sibling = (row, q + 1 - 2 * c)
 
@@ -127,52 +129,97 @@
 
         return wait
 
-    def scatter_start(ax, part, land):
-        copies = []
-        for m in range(2):
-            mate = (1 - ax.mate) if m == 0 else ax.mate
-            for d in (2, 1, 3):
-                ring = rem(ax.ring + d, 4)
-                copies.append(
-                    send(
-                        ax.pick(part, ax.index(ring, mate)),
-                        land.at[d - 1, m],
-                        ax.device(ax.index(ring, ax.mate)),
-                    )
+    class Scatter:
+        def __init__(self, ax, part, far, near, stage, mate_land):
+            self.ax, self.part, self.far, self.near = ax, part, far, near
+            self.stage, self.mate_land = stage, mate_land
+            self.far_copies, self.near_copies = [None, None], [None, None]
+
+        def at(self, d, m):
+            mate = (1 - self.ax.mate) if m == 0 else self.ax.mate
+            return self.ax.index(rem(self.ax.ring + d, 4), mate)
+
+        def next(self, d):
+            return self.ax.device(self.ax.index(rem(self.ax.ring + d, 4), self.ax.mate))
+
+        def start(self, m):
+            self.far_copies[m] = [
+                send(self.ax.half(self.part, self.at(2, m), h), self.far.at[m, h], self.next((1, 3)[h]))
+                for h in range(2)
+            ]
+
+        def step(self, m):
+            self.near_copies[m] = []
+            for h in range(2):
+                d = (1, 3)[h]
+                self.far_copies[m][h].wait_recv()
+                half = self.ax.half(self.part, self.at(d, m), h)
+                half[...] = half[...] + self.far[m, h]
+                self.near_copies[m].append(
+                    send(self.ax.pick(self.part, self.at(d, m)), self.near.at[m, h], self.next(d))
                 )
-        return copies
-
-    def scatter_mate(ax, part, land, copies, stage, mate_land):
-        for copy in copies[:3]:
-            copy.wait_recv()
-        stage[...] = (ax.pick(part, ax.index(ax.ring, 1 - ax.mate))[...] + land[0, 0]) + (land[1, 0] + land[2, 0])
-        return send(stage, mate_land, ax.device(ax.index(ax.ring, 1 - ax.mate)))
-
-    def scatter_end(ax, part, land, copies, mate_copy, mate_land):
-        for copy in copies[3:]:
-            copy.wait_recv()
-        value = (ax.pick(part, ax.me)[...] + land[0, 1]) + (land[1, 1] + land[2, 1])
-        mate_copy.wait_recv()
-        return value + mate_land[...]
-
-    def gather_start(ax, full):
-        piece = ax.pick(full, ax.me)
-        mate = send(piece, piece, ax.device(ax.index(ax.ring, 1 - ax.mate)))
-        copies = []
-        for d in (2, 1, 3):
-            copies.append(send(piece, piece, ax.device(ax.index(rem(ax.ring + d, 4), ax.mate))))
-        return mate, copies
-
-    def gather_forward(ax, full, started):
-        mate, copies = started
-        mate.wait_recv()
-        piece = ax.pick(full, ax.index(ax.ring, 1 - ax.mate))
-        for d in (2, 1, 3):
-            copies.append(send(piece, piece, ax.device(ax.index(rem(ax.ring + d, 4), ax.mate))))
-
-    def gather_end(started):
-        for copy in started[1]:
-            copy.wait_recv()
+
+        def total(self, m):
+            for copy in self.near_copies[m]:
+                copy.wait_recv()
+            return self.ax.pick(self.part, self.at(0, m))[...] + (self.near[m, 0] + self.near[m, 1])
+
+        def to_mate(self):
+            self.stage[...] = self.total(0)
+            self.mate_copy = send(self.stage, self.mate_land, self.ax.device(self.at(0, 0)))
+
+        def end(self):
+            value = self.total(1)
+            self.mate_copy.wait_recv()
+            return value + self.mate_land[...]
+
+        def copies(self):
+            return sum(self.far_copies + self.near_copies, []) + [self.mate_copy]
+
+    class Gather:
+        def __init__(self, ax, full, also=None):
+            self.ax, self.full = ax, full
+            self.also = also if also is not None else (lambda ref: None)
+
+        def at(self, d, m):
+            mate = (1 - self.ax.mate) if m == 0 else self.ax.mate
+            return self.ax.index(rem(self.ax.ring + d, 4), mate)
+
+        def both_ways(self, m):
+            piece = self.ax.pick(self.full, self.at(0, m))
+            self.also(piece)
+            return [send(piece, piece, self.ax.device(self.at(d, 1))) for d in (1, 3)]
+
+        def onward(self, m, copies):
+            out = []
+            for h in range(2):
+                copies[h].wait_recv()
+                i = self.at((3, 1)[h], m)
+                piece = self.ax.half(self.full, i, h)
+                out.append(send(piece, piece, self.ax.device(self.at((1, 3)[h], 1))))
+                self.also(self.ax.pick(self.full, i))
+            return out
+
+        def start(self):
+            piece = self.ax.pick(self.full, self.ax.me)
+            self.mate_copy = send(piece, piece, self.ax.device(self.at(0, 0)))
+            self.own = self.both_ways(1)
+
+        def step1(self):
+            self.own_far = self.onward(1, self.own)
+
+        def step2(self):
+            self.mate_copy.wait_recv()
+            self.other = self.both_ways(0)
+
+        def step3(self):
+            self.other_far = self.onward(0, self.other)
+
+        def end(self):
+            for m, copies in ((1, self.own_far), (0, self.other_far)):
+                for copy in copies:
+                    copy.wait_recv()
+                self.also(self.ax.pick(self.full, self.at(2, m)))
 
     def lanes(n, size):
         return pl.ds(pl.multiple_of(n * size, size), size)
@@ -180,17 +227,15 @@
     a_copy = send(a_ref.at[o], a_in, sibling)
     f_copy = send(f_ref, f_sib, sibling)
     f_hop1 = all_to_all(col_ax, lambda i: f_ref.at[i, row], lambda i: uf.at[i])
-    v_copy = send(v_ref.at[o], v_in, sibling)
-    v_hop1 = all_to_all(row_ax, lambda i: v_ref.at[:, i], lambda i: b1.at[i])
 
     fk_hl[0, c], fk_hl[1, c] = split(f_ref[...].reshape(512, 1024))
     lh[0, :, lanes(c, 512)], lh[1, :, lanes(c, 512)] = split(a_ref[c])
     a_copy.wait_recv()
     lh[0, :, lanes(o, 512)], lh[1, :, lanes(o, 512)] = split(a_in[...])
+    f_hop1()
+    f_hop2 = all_to_all(row_ax, lambda i: uf.at[i], lambda i: fr.at[c, k, i])
     f_copy.wait_recv()
     fk_hl[0, o], fk_hl[1, o] = split(f_sib[...].reshape(512, 1024))
-    f_hop1()
-    f_hop2 = all_to_all(row_ax, lambda i: uf.at[i], lambda i: fr.at[c, k, i])
 
     def product_nn(left, right, out):
         @pl.loop(0, 4)
@@ -203,18 +248,30 @@
             out[:, :, :, cols] = res.reshape(8, 8, 8, 256)
 
     product_nn(lh, fk_hl, pa)
-    rs0 = scatter_start(col_ax, pa, land_c)
+    rs0 = Scatter(col_ax, pa, far_c, near_c, sum_c, mate_c)
+    rs0.start(0)
+    rs0.start(1)
+    v_copy = send(v_ref.at[o], v_in, sibling)
     f_hop2()
-    f_gather = gather_start(col_ax, fr.at[c])
-    mate0 = scatter_mate(col_ax, pa, land_c, rs0, sum_c, mate_c)
-    i_own = scatter_end(col_ax, pa, land_c, rs0, mate0, mate_c)
-    inter[k] = i_own
-    i_gather = gather_start(col_ax, inter)
-    gather_forward(col_ax, inter, i_gather)
-    gather_forward(col_ax, fr.at[c], f_gather)
+    f_gather = Gather(col_ax, fr.at[c], lambda piece: f_also.append(send(piece, piece, sibling)))
+    f_also = []
+    f_gather.start()
+    rs0.step(0)
+    rs0.step(1)
+    v_hop1 = all_to_all(row_ax, lambda i: v_ref.at[:, i], lambda i: b1.at[i])
+    rs0.to_mate()
+    f_gather.step1()
+    inter[k] = rs0.end()
+    i_gather = Gather(col_ax, inter)
+    i_gather.start()
+    f_gather.step2()
+    i_gather.step1()
+    i_gather.step2()
+    f_gather.step3()
+    i_gather.step3()
     v_hop1()
+    i_gather.end()
     v_hop2 = all_to_all(col_ax, lambda i: b1.at[i], lambda i: b2.at[i])
-    gather_end(i_gather)
 
     lf[0], lf[1] = split(inter[...].reshape(512, 1024))
     v_copy.wait_recv()
@@ -241,11 +298,12 @@
         lh[0, :, at], lh[1, :, at] = split(y)
         lt[0, rows, lanes(c, 512)], lt[1, rows, lanes(c, 512)] = split(y.T)
 
-    sent(rs0)
+    sent(rs0.copies())
     product_nn(lh, fk_hl, pa)
-    rs1_c = scatter_start(col_ax, pa, land_c)
-    gather_end(f_gather)
-    f_copy2 = send(fr.at[c], fr.at[c], sibling)
+    rs1_c = Scatter(col_ax, pa, far_c, near_c, sum_c, mate_c)
+    rs1_c.start(0)
+    rs1_c.start(1)
+    f_gather.end()
     fr_hl[0, c], fr_hl[1, c] = split(fr[c].reshape(512, 1024))
     y_copy.wait_recv()
 
@@ -254,21 +312,25 @@
         rows = lanes(n, 256)
         lt[0, rows, lanes(o, 512)], lt[1, rows, lanes(o, 512)] = split(y_in[:, rows].T)
 
-    f_copy2.wait_recv()
+    rs1_c.step(0)
+    rs1_c.step(1)
+    for copy in f_also:
+        copy.wait_recv()
     fr_hl[0, o], fr_hl[1, o] = split(fr[o].reshape(512, 1024))
     product_nn(lt, fr_hl, pb)
-    rs1_r = scatter_start(row_ax, pb, land_r)
+    rs1_r = Scatter(row_ax, pb, far_r, near_r, sum_r, mate_r)
+    rs1_r.start(0)
+    rs1_r.start(1)
+    rs1_c.to_mate()
     v_hop2()
     v_hop3 = all_to_all(row_ax, lambda i: b2.at[i], lambda i: b3.at[i])
 
-    sent([mate0])
-    mate1_c = scatter_mate(col_ax, pa, land_c, rs1_c, sum_c, mate_c)
-    mate1_r = scatter_mate(row_ax, pb, land_r, rs1_r, sum_r, mate_r)
-    own_c[...] = (2.0 * KEEP * OMEGA) * i_own - (OMEGA * OMEGA) * scatter_end(
-        col_ax, pa, land_c, rs1_c, mate1_c, mate_c
-    )
+    rs1_r.step(0)
+    rs1_r.step(1)
+    own_c[...] = (2.0 * KEEP * OMEGA) * inter[k] - (OMEGA * OMEGA) * rs1_c.end()
     c_hop1 = all_to_all(row_ax, lambda i: own_c.at[i], lambda i: t1.at[i])
-    own_r[...] = -(OMEGA * OMEGA) * scatter_end(row_ax, pb, land_r, rs1_r, mate1_r, mate_r)
+    rs1_r.to_mate()
+    own_r[...] = -(OMEGA * OMEGA) * rs1_r.end()
     r_hop1 = all_to_all(col_ax, lambda i: own_r.at[i], lambda i: u1.at[i])
     c_hop1()
     c_hop2 = all_to_all(col_ax, lambda i: t1.at[i], lambda i: t2.at[i])
@@ -276,18 +338,24 @@
     r_hop2 = all_to_all(row_ax, lambda i: u1.at[i], lambda i: u2.at[i])
     c_hop2()
     row_ax.pick(wk, row)[...] = own_r[...] + t2[...]
-    k_gather = gather_start(row_ax, wk)
+    k_gather = Gather(row_ax, wk)
+    k_gather.start()
     r_hop2()
     wr[c, k] = own_c[...] + u2[...]
-    r_gather = gather_start(col_ax, wr.at[c])
-    gather_forward(row_ax, wk, k_gather)
-    gather_forward(col_ax, wr.at[c], r_gather)
+    r_gather = Gather(col_ax, wr.at[c])
+    r_gather.start()
+    k_gather.step1()
+    r_gather.step1()
+    k_gather.step2()
+    r_gather.step2()
+    k_gather.step3()
+    r_gather.step3()
     v_hop3()
     vt_copy = send(b3.at[:, o], vt_sib, sibling)
-    gather_end(r_gather)
+    r_gather.end()
     w_copy = send(wr.at[c], wr.at[c], sibling)
     lf[0], lf[1] = split(wr[c].reshape(512, 1024))
-    gather_end(k_gather)
+    k_gather.end()
     lt[0], lt[1] = split(wk[...].reshape(512, 1024))
 
     def finish(half, mirrored):
@@ -336,8 +404,10 @@
             half(2, 2, 512, 1024),
             big(8, 8, 8, 1024),
             big(8, 8, 8, 1024),
-            big(3, 2, 8, 8, 1024),
-            big(3, 2, 8, 8, 1024),
+            big(2, 2, 4, 8, 1024),
+            big(2, 2, 8, 8, 1024),
+            big(2, 2, 4, 8, 1024),
+            big(2, 2, 8, 8, 1024),
             big(8, 8, 1024),
             big(8, 8, 1024),
             big(8, 8, 1024),

time: 221 us -> 223 us (level)
  no operation moved by 1% of the time
where the time goes in v2:
time: 223 us; the launch traced here: 222 us
  Pallas kernels  215 us (96%)
  local copies, waits for them, and re-layouts  5.57 us (2%)
    pallas_call x1, Pallas kernels, on_device(): pl.pallas_call(kernel, out_shape=jax.ShapeDtypeStruct((2, 512, 512), F32)...  215 us

profile of v2, /device:TPU:1, one launch (start us, length us, event | category | flops | bytes accessed | tf_op | source)
XLA Modules:
  0.0 222.3 jit_solution(7965395711306409369)
XLA Ops:
  0.0 0.8 fusion.1
  0.8 0.8 select_reduce_fusion.1
  1.6 1.3 select_reduce_fusion
  2.9 0.6 fusion.2
  3.5 1.1 slice.18.er_ref
  4.6 214.6 %lambda_steps.1 = f32[2,512,512]{2,1,0:T(8,128)} custom-call(f32[2,512,512]{2,1,0:T(8,128)} %bitcast.6, f32[2,8,64,512]{3,2,1,0:T(8,128)} %bitcast.7, f32[8,8,8,1024]{3,2,1,0:T(8,128)} %bitcast.8, f32[2,512,1]{2,1,0:T(8,128)} %slice.18.er_ref, f32[2,1,512]{2,1,0:T(1,128)} %bitcast.9), custom_call_target="tpu_custom_call" | custom-call | tf_op jit(solution)/shard_map/lambda_steps/pallas_call | solution.py:393
  219.2 3.1 %copy.10 = f32[1024,512]{1,0:T(8,128)} copy(f32[1024,512]{1,0:T(8,128)} %bitcast.5) | data formatting | bytes 4194304
  (2 shorter events, 0.0 us)

commit v3 on v2

--- a/solution.py
+++ b/solution.py
@@ -57,10 +57,11 @@
 
 def kernel(
     a_ref, v_ref, f_ref, er_ref, ec_ref, o_ref,
-    a_in, v_in, f_sib, fk_hl, fr, fr_hl, pa, pb, far_c, near_c, far_r, near_r, mate_c, mate_r,
-    sum_c, sum_r, own_c, own_r, inter, y_out, y_in, lh, lf, lt, wr, wk,
-    b1, b2, b3, vt_sib, t1, t2, u1, u2, uf, ss, rs, ls,
+    a_in, v_in, f_sib, fk_hl, fr, fr_hl, pa, far_c, near_c, far_r, near_r, mate_c, mate_r,
+    sum_c, sum_r, own_c, own_r, inter, y_in, lh, lf, lt, wr, wk,
+    b1, b2, b3, vt_sib, t1, t2, u1, u2, fg, ss, rs, ls,
 ):
+    pb, y_out = f_sib, a_in
     row = lax.axis_index("row")
     q = lax.axis_index("col")
     c = rem(q, 2)
@@ -177,9 +178,8 @@
             return sum(self.far_copies + self.near_copies, []) + [self.mate_copy]
 
     class Gather:
-        def __init__(self, ax, full, also=None):
+        def __init__(self, ax, full):
             self.ax, self.full = ax, full
-            self.also = also if also is not None else (lambda ref: None)
 
         def at(self, d, m):
             mate = (1 - self.ax.mate) if m == 0 else self.ax.mate
@@ -187,7 +187,6 @@
 
         def both_ways(self, m):
             piece = self.ax.pick(self.full, self.at(0, m))
-            self.also(piece)
             return [send(piece, piece, self.ax.device(self.at(d, 1))) for d in (1, 3)]
 
         def onward(self, m, copies):
@@ -197,7 +196,6 @@
                 i = self.at((3, 1)[h], m)
                 piece = self.ax.half(self.full, i, h)
                 out.append(send(piece, piece, self.ax.device(self.at((1, 3)[h], 1))))
-                self.also(self.ax.pick(self.full, i))
             return out
 
         def start(self):
@@ -216,26 +214,28 @@
             self.other_far = self.onward(0, self.other)
 
         def end(self):
-            for m, copies in ((1, self.own_far), (0, self.other_far)):
-                for copy in copies:
-                    copy.wait_recv()
-                self.also(self.ax.pick(self.full, self.at(2, m)))
+            for copy in self.own_far + self.other_far:
+                copy.wait_recv()
 
     def lanes(n, size):
         return pl.ds(pl.multiple_of(n * size, size), size)
 
     a_copy = send(a_ref.at[o], a_in, sibling)
     f_copy = send(f_ref, f_sib, sibling)
-    f_hop1 = all_to_all(col_ax, lambda i: f_ref.at[i, row], lambda i: uf.at[i])
+    f_mine = local(f_ref.at[row], fg.at[k])
+    f_mine.wait()
+    f_gather = Gather(col_ax, fg)
+    f_gather.start()
+    v_hop1 = all_to_all(row_ax, lambda i: v_ref.at[:, i], lambda i: b1.at[i])
 
     fk_hl[0, c], fk_hl[1, c] = split(f_ref[...].reshape(512, 1024))
     lh[0, :, lanes(c, 512)], lh[1, :, lanes(c, 512)] = split(a_ref[c])
     a_copy.wait_recv()
     lh[0, :, lanes(o, 512)], lh[1, :, lanes(o, 512)] = split(a_in[...])
-    f_hop1()
-    f_hop2 = all_to_all(row_ax, lambda i: uf.at[i], lambda i: fr.at[c, k, i])
     f_copy.wait_recv()
     fk_hl[0, o], fk_hl[1, o] = split(f_sib[...].reshape(512, 1024))
+    f_gather.step1()
+    f_gather.step2()
 
     def product_nn(left, right, out):
         @pl.loop(0, 4)
@@ -252,22 +252,17 @@
     rs0.start(0)
     rs0.start(1)
     v_copy = send(v_ref.at[o], v_in, sibling)
-    f_hop2()
-    f_gather = Gather(col_ax, fr.at[c], lambda piece: f_also.append(send(piece, piece, sibling)))
-    f_also = []
-    f_gather.start()
     rs0.step(0)
     rs0.step(1)
-    v_hop1 = all_to_all(row_ax, lambda i: v_ref.at[:, i], lambda i: b1.at[i])
+    f_gather.step3()
     rs0.to_mate()
-    f_gather.step1()
     inter[k] = rs0.end()
     i_gather = Gather(col_ax, inter)
     i_gather.start()
-    f_gather.step2()
+    f_gather.end()
+    f_hop = all_to_all(row_ax, lambda i: fg.at[i], lambda i: fr.at[c, i])
     i_gather.step1()
     i_gather.step2()
-    f_gather.step3()
     i_gather.step3()
     v_hop1()
     i_gather.end()
@@ -303,7 +298,8 @@
     rs1_c = Scatter(col_ax, pa, far_c, near_c, sum_c, mate_c)
     rs1_c.start(0)
     rs1_c.start(1)
-    f_gather.end()
+    f_hop()
+    f_copy2 = send(fr.at[c], fr.at[c], sibling)
     fr_hl[0, c], fr_hl[1, c] = split(fr[c].reshape(512, 1024))
     y_copy.wait_recv()
 
@@ -314,19 +310,18 @@
 
     rs1_c.step(0)
     rs1_c.step(1)
-    for copy in f_also:
-        copy.wait_recv()
+    f_copy2.wait_recv()
     fr_hl[0, o], fr_hl[1, o] = split(fr[o].reshape(512, 1024))
     product_nn(lt, fr_hl, pb)
     rs1_r = Scatter(row_ax, pb, far_r, near_r, sum_r, mate_r)
     rs1_r.start(0)
     rs1_r.start(1)
     rs1_c.to_mate()
+
+    rs1_r.step(0)
+    rs1_r.step(1)
     v_hop2()
     v_hop3 = all_to_all(row_ax, lambda i: b2.at[i], lambda i: b3.at[i])
-
-    rs1_r.step(0)
-    rs1_r.step(1)
     own_c[...] = (2.0 * KEEP * OMEGA) * inter[k] - (OMEGA * OMEGA) * rs1_c.end()
     c_hop1 = all_to_all(row_ax, lambda i: own_c.at[i], lambda i: t1.at[i])
     rs1_r.to_mate()
@@ -403,7 +398,6 @@
             big(2, 8, 8, 8, 1024),
             half(2, 2, 512, 1024),
             big(8, 8, 8, 1024),
-            big(8, 8, 8, 1024),
             big(2, 2, 4, 8, 1024),
             big(2, 2, 8, 8, 1024),
             big(2, 2, 4, 8, 1024),
@@ -415,7 +409,6 @@
             big(8, 8, 1024),
             big(8, 8, 1024),
             big(8, 8, 8, 1024),
-            big(512, 512),
             big(512, 512),
             half(2, 512, 1024),
             half(2, 512, 1024),
@@ -430,7 +423,7 @@
             big(8, 8, 1024),
             big(8, 8, 1024),
             big(8, 8, 1024),
-            big(8, 8, 1024),
+            big(8, 8, 8, 1024),
             pltpu.SemaphoreType.DMA((N_SEM,)),
             pltpu.SemaphoreType.DMA((N_SEM,)),
             pltpu.SemaphoreType.DMA((16,)),

time: 223 us -> 212 us (0.951)
  Pallas kernels: 215 us -> 204 us
    pallas_call x1, Pallas kernels: 215 us -> 204 us  [on_device(): pl.pallas_call(kernel, out_shape=jax.ShapeDtypeStruct((2, 512, 512), F32)...]
where the time goes in v3:
time: 212 us
  Pallas kernels  204 us (96%)
  local copies, waits for them, and re-layouts  5.57 us (3%)
  other arithmetic  2.12 us (1%)
    pallas_call x1, Pallas kernels, on_device(): pl.pallas_call(kernel, out_shape=jax.ShapeDtypeStruct((2, 512, 512), F32)...  204 us

profile of v3, /device:TPU:1, one launch (start us, length us, event | category | flops | bytes accessed | tf_op | source)
XLA Modules:
  0.0 211.7 jit_solution(10656329989586694424)
XLA Ops:
  0.0 0.8 fusion.1
  0.8 0.8 select_reduce_fusion.1
  1.6 1.3 select_reduce_fusion
  2.9 0.6 fusion.2
  3.5 1.1 slice.18.er_ref
  4.6 204.0 %lambda_steps.1 = f32[2,512,512]{2,1,0:T(8,128)} custom-call(f32[2,512,512]{2,1,0:T(8,128)} %bitcast.6, f32[2,8,64,512]{3,2,1,0:T(8,128)} %bitcast.7, f32[8,8,8,1024]{3,2,1,0:T(8,128)} %bitcast.8, f32[2,512,1]{2,1,0:T(8,128)} %slice.18.er_ref, f32[2,1,512]{2,1,0:T(1,128)} %bitcast.9), custom_call_target="tpu_custom_call" | custom-call | tf_op jit(solution)/shard_map/lambda_steps/pallas_call | solution.py:388
  208.6 3.1 %copy.10 = f32[1024,512]{1,0:T(8,128)} copy(f32[1024,512]{1,0:T(8,128)} %bitcast.5) | data formatting | bytes 4194304
  (2 shorter events, 0.0 us)

commit v4 on v3

--- a/solution.py
+++ b/solution.py
@@ -13,14 +13,17 @@
 MESH = pl.DeviceIdType.MESH
 F32 = jnp.float32
 BF16 = jnp.bfloat16
-N_SEM = 160
-
-
-def pair_energy(pair_order, occ_energy, vir_energy):
-    occ_hit = (pair_order // NV)[:, None] == jnp.arange(NO, dtype=jnp.int32)[None, :]
-    vir_hit = (pair_order % NV)[:, None] == jnp.arange(NV, dtype=jnp.int32)[None, :]
-    return jnp.sum(jnp.where(vir_hit, vir_energy[None, :], 0.0), axis=1) - jnp.sum(
-        jnp.where(occ_hit, occ_energy[None, :], 0.0), axis=1
+N_SEM = 232
+
+
+def pair_energy(codes, occ, vir):
+    n = codes.shape[1]
+    at_occ = lax.broadcasted_iota(jnp.int32, (NO, n), 0)
+    at_vir = lax.broadcasted_iota(jnp.int32, (NV, n), 0)
+    occ_hit = at_occ == lax.shift_right_logical(codes, jnp.int32(7))
+    vir_hit = at_vir == (codes & (NV - 1))
+    return jnp.sum(jnp.where(vir_hit, vir, 0.0), axis=0, keepdims=True) - jnp.sum(
+        jnp.where(occ_hit, occ, 0.0), axis=0, keepdims=True
     )
 
 
@@ -56,10 +59,10 @@
 
 
 def kernel(
-    a_ref, v_ref, f_ref, er_ref, ec_ref, o_ref,
+    a_ref, v_ref, f_ref, order_ref, occ_ref, vir_ref, o_ref,
     a_in, v_in, f_sib, fk_hl, fr, fr_hl, pa, far_c, near_c, far_r, near_r, mate_c, mate_r,
     sum_c, sum_r, own_c, own_r, inter, y_in, lh, lf, lt, wr, wk,
-    b1, b2, b3, vt_sib, t1, t2, u1, u2, fg, ss, rs, ls,
+    b1, b2, b3, vt_sib, t1, t2, u1, u2, fg, er_ref, ec_ref, ss, rs, ls, fs,
 ):
     pb, y_out = f_sib, a_in
     row = lax.axis_index("row")
@@ -88,6 +91,17 @@
         for d in range(1, 8):
             pl.semaphore_signal(barrier, inc=1, device_id=ax.device(rem(ax.me + d, 8)), device_id_type=MESH)
     pl.semaphore_signal(barrier, inc=1, device_id=sibling, device_id_type=MESH)
+
+    def energies(start):
+        return pair_energy(
+            order_ref[:, pl.ds(pl.multiple_of(start, 1024), 1024)], occ_ref[...], vir_ref[...]
+        )
+
+    row_energy, col_energy = energies(row * 1024), energies(k * 1024)
+    for h in range(2):
+        mine = row_energy[:, h * 512 : (h + 1) * 512]
+        er_ref[h] = jnp.broadcast_to(mine, (128, 512)).T
+        ec_ref[h] = col_energy[:, h * 512 : (h + 1) * 512]
     pl.semaphore_wait(barrier, 15)
 
     used = [0, 0]
@@ -178,8 +192,9 @@
             return sum(self.far_copies + self.near_copies, []) + [self.mate_copy]
 
     class Gather:
-        def __init__(self, ax, full):
+        def __init__(self, ax, full, also=None):
             self.ax, self.full = ax, full
+            self.also = also if also is not None else (lambda i: None)
 
         def at(self, d, m):
             mate = (1 - self.ax.mate) if m == 0 else self.ax.mate
@@ -187,6 +202,7 @@
 
         def both_ways(self, m):
             piece = self.ax.pick(self.full, self.at(0, m))
+            self.also(self.at(0, m))
             return [send(piece, piece, self.ax.device(self.at(d, 1))) for d in (1, 3)]
 
         def onward(self, m, copies):
@@ -196,6 +212,7 @@
                 i = self.at((3, 1)[h], m)
                 piece = self.ax.half(self.full, i, h)
                 out.append(send(piece, piece, self.ax.device(self.at((1, 3)[h], 1))))
+                self.also(i)
             return out
 
         def start(self):
@@ -214,8 +231,10 @@
             self.other_far = self.onward(0, self.other)
 
         def end(self):
-            for copy in self.own_far + self.other_far:
-                copy.wait_recv()
+            for m, copies in ((1, self.own_far), (0, self.other_far)):
+                for copy in copies:
+                    copy.wait_recv()
+                self.also(self.at(2, m))
 
     def lanes(n, size):
         return pl.ds(pl.multiple_of(n * size, size), size)
@@ -224,7 +243,30 @@
     f_copy = send(f_ref, f_sib, sibling)
     f_mine = local(f_ref.at[row], fg.at[k])
     f_mine.wait()
-    f_gather = Gather(col_ax, fg)
+    moves = []
+
+    def move(i):
+        n = used[0]
+        used[0] += 1
+        far = pltpu.make_async_remote_copy(
+            src_ref=fg.at[i], dst_ref=fr.at[c, row], send_sem=ss.at[n], recv_sem=fs.at[row],
+            device_id=row_ax.device(i), device_id_type=MESH,
+        )
+        near = pltpu.make_async_copy(fg.at[i], fr.at[c, row], fs.at[8])
+        pl.when(i != row)(far.start)
+        pl.when(i == row)(near.start)
+        moves.append((i, far, near))
+
+    def moved():
+        moves[0][2].wait()
+        for j in range(8):
+            come = pltpu.make_async_remote_copy(
+                src_ref=fg.at[j], dst_ref=fr.at[c, j], send_sem=fs.at[9], recv_sem=fs.at[j],
+                device_id=row_ax.device(jnp.int32(j)), device_id_type=MESH,
+            )
+            pl.when(row != j)(come.wait_recv)
+
+    f_gather = Gather(col_ax, fg, move)
     f_gather.start()
     v_hop1 = all_to_all(row_ax, lambda i: v_ref.at[:, i], lambda i: b1.at[i])
 
@@ -237,38 +279,55 @@
     f_gather.step1()
     f_gather.step2()
 
-    def product_nn(left, right, out):
-        @pl.loop(0, 4)
+    def chunk(ref, h):
+        return ref.at[(slice(None),) * (len(ref.shape) - 1) + (pl.ds(h * 512, 512),)]
+
+    def product_nn(left, right, out, h):
+        @pl.loop(0, 2)
         def _(n):
-            cols = lanes(n, 256)
+            cols = pl.ds(pl.multiple_of(h * 512 + n * 256, 256), 256)
             res = triple(
                 dot_nn, left[0], left[1],
                 right[0, :, :, cols].reshape(1024, 256), right[1, :, :, cols].reshape(1024, 256),
             )
             out[:, :, :, cols] = res.reshape(8, 8, 8, 256)
 
-    product_nn(lh, fk_hl, pa)
-    rs0 = Scatter(col_ax, pa, far_c, near_c, sum_c, mate_c)
-    rs0.start(0)
-    rs0.start(1)
+    def scatters(ax, part, far, near, stage, mate_land):
+        return [
+            Scatter(ax, chunk(part, h), far.at[h], near.at[h], stage.at[h], mate_land.at[h]) for h in range(2)
+        ]
+
+    rs0 = scatters(col_ax, pa, far_c, near_c, sum_c, mate_c)
+    i_gather = [Gather(col_ax, chunk(inter, h)) for h in range(2)]
+    for h in range(2):
+        product_nn(lh, fk_hl, pa, h)
+        rs0[h].start(0)
+        rs0[h].start(1)
+    f_gather.step3()
     v_copy = send(v_ref.at[o], v_in, sibling)
-    rs0.step(0)
-    rs0.step(1)
-    f_gather.step3()
-    rs0.to_mate()
-    inter[k] = rs0.end()
-    i_gather = Gather(col_ax, inter)
-    i_gather.start()
+    for h in range(2):
+        rs0[h].step(0)
+        rs0[h].step(1)
     f_gather.end()
-    f_hop = all_to_all(row_ax, lambda i: fg.at[i], lambda i: fr.at[c, i])
-    i_gather.step1()
-    i_gather.step2()
-    i_gather.step3()
+    for h in range(2):
+        rs0[h].to_mate()
+        chunk(inter, h)[k] = rs0[h].end()
+        i_gather[h].start()
+    for h in range(2):
+        i_gather[h].step1()
+        i_gather[h].step2()
+    i_gather[0].step3()
     v_hop1()
-    i_gather.end()
+    i_gather[0].end()
+    lf[0, :, :512], lf[1, :, :512] = split(inter[:, :, :, :512].reshape(512, 512))
+    i_gather[1].step3()
+    moved()
+    f_copy2 = send(fr.at[c], fr.at[c], sibling)
+    fr_hl[0, c], fr_hl[1, c] = split(fr[c].reshape(512, 1024))
+    i_gather[1].end()
     v_hop2 = all_to_all(col_ax, lambda i: b1.at[i], lambda i: b2.at[i])
-
-    lf[0], lf[1] = split(inter[...].reshape(512, 1024))
+    lf[0, :, 512:], lf[1, :, 512:] = split(inter[:, :, :, 512:].reshape(512, 512))
+
     v_copy.wait_recv()
 
     @pl.loop(0, 2)
@@ -276,7 +335,7 @@
         rows = lanes(n, 256)
         res = triple(dot_nt, lf[0], lf[1], fk_hl[0, o, rows], fk_hl[1, o, rows])
         drive = v_in[:, :, rows].reshape(512, 256)
-        y = (drive + res) / (er_ref[c] + ec_ref[o, :, rows])
+        y = (drive + res) / (er_ref[c, :, :1] + ec_ref[o, :, rows])
         y_out[:, rows] = y
         at = pl.ds(pl.multiple_of(o * 512 + n * 256, 256), 256)
         lh[0, :, at], lh[1, :, at] = split(y)
@@ -288,19 +347,18 @@
         rows = lanes(n, 256)
         res = triple(dot_nt, lf[0], lf[1], fk_hl[0, c, rows], fk_hl[1, c, rows])
         drive = v_ref[c, :, :, rows].reshape(512, 256)
-        y = (drive + res) / (er_ref[c] + ec_ref[c, :, rows])
+        y = (drive + res) / (er_ref[c, :, :1] + ec_ref[c, :, rows])
         at = pl.ds(pl.multiple_of(c * 512 + n * 256, 256), 256)
         lh[0, :, at], lh[1, :, at] = split(y)
         lt[0, rows, lanes(c, 512)], lt[1, rows, lanes(c, 512)] = split(y.T)
 
-    sent(rs0.copies())
-    product_nn(lh, fk_hl, pa)
-    rs1_c = Scatter(col_ax, pa, far_c, near_c, sum_c, mate_c)
-    rs1_c.start(0)
-    rs1_c.start(1)
-    f_hop()
-    f_copy2 = send(fr.at[c], fr.at[c], sibling)
-    fr_hl[0, c], fr_hl[1, c] = split(fr[c].reshape(512, 1024))
+    sent(rs0[0].copies() + rs0[1].copies())
+    rs1_c = scatters(col_ax, pa, far_c, near_c, sum_c, mate_c)
+    rs1_r = scatters(row_ax, pb, far_r, near_r, sum_r, mate_r)
+    for h in range(2):
+        product_nn(lh, fk_hl, pa, h)
+        rs1_c[h].start(0)
+        rs1_c[h].start(1)
     y_copy.wait_recv()
 
     @pl.loop(0, 2)
@@ -308,87 +366,134 @@
         rows = lanes(n, 256)
         lt[0, rows, lanes(o, 512)], lt[1, rows, lanes(o, 512)] = split(y_in[:, rows].T)
 
-    rs1_c.step(0)
-    rs1_c.step(1)
     f_copy2.wait_recv()
     fr_hl[0, o], fr_hl[1, o] = split(fr[o].reshape(512, 1024))
-    product_nn(lt, fr_hl, pb)
-    rs1_r = Scatter(row_ax, pb, far_r, near_r, sum_r, mate_r)
-    rs1_r.start(0)
-    rs1_r.start(1)
-    rs1_c.to_mate()
-
-    rs1_r.step(0)
-    rs1_r.step(1)
+    for h in range(2):
+        product_nn(lt, fr_hl, pb, h)
+        rs1_r[h].start(0)
+        rs1_r[h].start(1)
+        rs1_c[h].step(0)
+        rs1_c[h].step(1)
+
+    c_hop1, r_hop1, c_hop2, r_hop2 = [None] * 2, [None] * 2, [None] * 2, [None] * 2
+    k_gather = [Gather(row_ax, chunk(wk, h)) for h in range(2)]
+    r_gather = [Gather(col_ax, chunk(wr.at[c], h)) for h in range(2)]
+
+    def end_c(h):
+        own_c[h] = (2.0 * KEEP * OMEGA) * chunk(inter, h)[k] - (OMEGA * OMEGA) * rs1_c[h].end()
+        c_hop1[h] = all_to_all(row_ax, lambda i: own_c.at[h, i], lambda i: t1.at[h, i])
+
+    def end_r(h):
+        own_r[h] = -(OMEGA * OMEGA) * rs1_r[h].end()
+        r_hop1[h] = all_to_all(col_ax, lambda i: own_r.at[h, i], lambda i: u1.at[h, i])
+
+    def second_hops(h):
+        c_hop1[h]()
+        c_hop2[h] = all_to_all(col_ax, lambda i: t1.at[h, i], lambda i: t2.at[h, i])
+        r_hop1[h]()
+        r_hop2[h] = all_to_all(row_ax, lambda i: u1.at[h, i], lambda i: u2.at[h, i])
+
+    def start_gathers(h):
+        c_hop2[h]()
+        row_ax.pick(chunk(wk, h), row)[...] = own_r[h] + t2[h]
+        k_gather[h].start()
+        r_hop2[h]()
+        col_ax.pick(chunk(wr.at[c], h), k)[...] = own_c[h] + u2[h]
+        r_gather[h].start()
+
+    rs1_r[0].step(0)
+    rs1_c[0].to_mate()
+    rs1_r[0].step(1)
+    rs1_c[1].to_mate()
+    rs1_r[1].step(0)
+    rs1_r[1].step(1)
+    end_c(0)
+    rs1_r[0].to_mate()
+    end_r(0)
+    end_c(1)
+    rs1_r[1].to_mate()
     v_hop2()
     v_hop3 = all_to_all(row_ax, lambda i: b2.at[i], lambda i: b3.at[i])
-    own_c[...] = (2.0 * KEEP * OMEGA) * inter[k] - (OMEGA * OMEGA) * rs1_c.end()
-    c_hop1 = all_to_all(row_ax, lambda i: own_c.at[i], lambda i: t1.at[i])
-    rs1_r.to_mate()
-    own_r[...] = -(OMEGA * OMEGA) * rs1_r.end()
-    r_hop1 = all_to_all(col_ax, lambda i: own_r.at[i], lambda i: u1.at[i])
-    c_hop1()
-    c_hop2 = all_to_all(col_ax, lambda i: t1.at[i], lambda i: t2.at[i])
-    r_hop1()
-    r_hop2 = all_to_all(row_ax, lambda i: u1.at[i], lambda i: u2.at[i])
-    c_hop2()
-    row_ax.pick(wk, row)[...] = own_r[...] + t2[...]
-    k_gather = Gather(row_ax, wk)
-    k_gather.start()
-    r_hop2()
-    wr[c, k] = own_c[...] + u2[...]
-    r_gather = Gather(col_ax, wr.at[c])
-    r_gather.start()
-    k_gather.step1()
-    r_gather.step1()
-    k_gather.step2()
-    r_gather.step2()
-    k_gather.step3()
-    r_gather.step3()
+    second_hops(0)
+    end_r(1)
+    start_gathers(0)
+    second_hops(1)
+    for gather in (k_gather[0], r_gather[0]):
+        gather.step1()
+        gather.step2()
+    start_gathers(1)
+    k_gather[0].step3()
+    r_gather[0].step3()
+    for gather in (k_gather[1], r_gather[1]):
+        gather.step1()
+        gather.step2()
+
+    def take(h):
+        cols = pl.ds(h * 512, 512)
+        copy = send(chunk(wr.at[c], h), chunk(wr.at[c], h), sibling)
+        lf[0, :, cols], lf[1, :, cols] = split(wr[c, :, :, :, cols].reshape(512, 512))
+        lt[0, :, cols], lt[1, :, cols] = split(wk[:, :, :, cols].reshape(512, 512))
+        return copy
+
+    def take_sibling(h, copy):
+        cols = pl.ds(h * 512, 512)
+        copy.wait_recv()
+        lh[0, :, cols], lh[1, :, cols] = split(wr[o, :, :, :, cols].reshape(512, 512))
+
+    def terms(half, left, n, h):
+        rows, cols = lanes(n, 256), pl.ds(h * 512, 512)
+        return triple(
+            dot_nt, left[0, :, cols], left[1, :, cols], fk_hl[0, c, rows, cols], fk_hl[1, c, rows, cols]
+        ) + triple(
+            dot_nt, fr_hl[0, half, :, cols], fr_hl[1, half, :, cols], lt[0, rows, cols], lt[1, rows, cols]
+        )
+
+    def first(half, left):
+        @pl.loop(0, 2)
+        def _(n):
+            o_ref[half, :, lanes(n, 256)] = terms(half, left, n, 0)
+
+    k_gather[0].end()
+    r_gather[0].end()
+    w_copy = take(0)
+    k_gather[1].step3()
+    r_gather[1].step3()
+    first(c, lf)
+    take_sibling(0, w_copy)
+    first(o, lh)
     v_hop3()
     vt_copy = send(b3.at[:, o], vt_sib, sibling)
-    r_gather.end()
-    w_copy = send(wr.at[c], wr.at[c], sibling)
-    lf[0], lf[1] = split(wr[c].reshape(512, 1024))
-    k_gather.end()
-    lt[0], lt[1] = split(wk[...].reshape(512, 1024))
-
-    def finish(half, mirrored):
+    k_gather[1].end()
+    r_gather[1].end()
+    w_copy = take(1)
+
+    def finish(half, left, mirrored):
         @pl.loop(0, 2)
         def _(n):
             rows = lanes(n, 256)
-            res = triple(dot_nt, lf[0], lf[1], fk_hl[0, c, rows], fk_hl[1, c, rows])
-            res = res + triple(dot_nt, fr_hl[0, half], fr_hl[1, half], lt[0, rows], lt[1, rows])
+            res = o_ref[half, :, rows] + terms(half, left, n, 1)
             drive = v_ref[half, :, :, rows].reshape(512, 256) + mirrored(n).reshape(256, 512).T
             sym = (1.0 + KEEP) * OMEGA * drive + res
             o_ref[half, :, rows] = (KEEP * KEEP) * a_ref[half, :, rows] - sym / (
-                er_ref[half] + ec_ref[c, :, rows]
+                er_ref[half, :, :1] + ec_ref[c, :, rows]
             )
 
-    finish(c, lambda n: b3[pl.ds(n * 4, 4), c])
-    w_copy.wait_recv()
-    lf[0], lf[1] = split(wr[o].reshape(512, 1024))
+    finish(c, lf, lambda n: b3[pl.ds(n * 4, 4), c])
+    take_sibling(1, w_copy)
     vt_copy.wait_recv()
-    finish(o, lambda n: vt_sib[pl.ds(n * 4, 4)])
+    finish(o, lh, lambda n: vt_sib[pl.ds(n * 4, 4)])
     sent(list(pending.values()))
+    for i, far, _ in moves:
+        pl.when(i != row)(far.wait_send)
 
 
 def on_device(amplitudes, integrals, factors, pair_order, occ_energy, vir_energy):
-    row = lax.axis_index("row")
-    q = lax.axis_index("col")
-    order = jnp.concatenate(
-        [
-            lax.dynamic_slice_in_dim(pair_order, row * 1024, 1024, 0),
-            lax.dynamic_slice_in_dim(pair_order, (q // 2) * 1024, 1024, 0),
-        ]
-    )
-    energy = pair_energy(order, occ_energy, vir_energy)
     big = lambda *shape: pltpu.VMEM(shape, F32)
     half = lambda *shape: pltpu.VMEM(shape, BF16)
     out = pl.pallas_call(
         kernel,
         out_shape=jax.ShapeDtypeStruct((2, 512, 512), F32),
-        in_specs=[pl.BlockSpec(memory_space=pltpu.VMEM)] * 5,
+        in_specs=[pl.BlockSpec(memory_space=pltpu.VMEM)] * 6,
         out_specs=pl.BlockSpec(memory_space=pltpu.VMEM),
         scratch_shapes=[
             big(512, 512),
@@ -398,16 +503,16 @@
             big(2, 8, 8, 8, 1024),
             half(2, 2, 512, 1024),
             big(8, 8, 8, 1024),
-            big(2, 2, 4, 8, 1024),
-            big(2, 2, 8, 8, 1024),
-            big(2, 2, 4, 8, 1024),
-            big(2, 2, 8, 8, 1024),
-            big(8, 8, 1024),
-            big(8, 8, 1024),
-            big(8, 8, 1024),
-            big(8, 8, 1024),
-            big(8, 8, 1024),
-            big(8, 8, 1024),
+            big(2, 2, 2, 4, 8, 512),
+            big(2, 2, 2, 8, 8, 512),
+            big(2, 2, 2, 4, 8, 512),
+            big(2, 2, 2, 8, 8, 512),
+            big(2, 8, 8, 512),
+            big(2, 8, 8, 512),
+            big(2, 8, 8, 512),
+            big(2, 8, 8, 512),
+            big(2, 8, 8, 512),
+            big(2, 8, 8, 512),
             big(8, 8, 8, 1024),
             big(512, 512),
             half(2, 512, 1024),
@@ -419,14 +524,17 @@
             big(8, 2, 64, 512),
             big(8, 2, 64, 512),
             big(8, 64, 512),
-            big(8, 8, 1024),
-            big(8, 8, 1024),
-            big(8, 8, 1024),
-            big(8, 8, 1024),
+            big(2, 8, 8, 512),
+            big(2, 8, 8, 512),
+            big(2, 8, 8, 512),
+            big(2, 8, 8, 512),
             big(8, 8, 8, 1024),
+            big(2, 512, 128),
+            big(2, 1, 512),
             pltpu.SemaphoreType.DMA((N_SEM,)),
             pltpu.SemaphoreType.DMA((N_SEM,)),
             pltpu.SemaphoreType.DMA((16,)),
+            pltpu.SemaphoreType.DMA((10,)),
         ],
         compiler_params=pltpu.CompilerParams(
             collective_id=0, has_side_effects=True, vmem_limit_bytes=63 * 2**20
@@ -436,8 +544,9 @@
         amplitudes.reshape(2, 512, 512),
         integrals.reshape(2, 8, 64, 512),
         factors.reshape(8, 8, 8, 1024),
-        energy[:1024].reshape(2, 512, 1),
-        energy[1024:].reshape(2, 1, 512),
+        pair_order.reshape(1, NO * NV),
+        occ_energy.reshape(NO, 1),
+        vir_energy.reshape(NV, 1),
     )
     return out.reshape(1024, 512)
 

time: 212 us -> 232 us (1.094)
  Pallas kernels: 204 us -> 226 us
    pallas_call x1, Pallas kernels: 204 us -> 226 us  [on_device(): pl.pallas_call(kernel, out_shape=jax.ShapeDtypeStruct((2, 512, 512), F32)...]
    reshape x0 -> x2, local copies, waits for them, and re-layouts: none -> 2.73 us  [the longest x1 1.39 us: on_device(): vir_energy.reshape(NV, 1)]
where the time goes in v4:
time: 232 us; the launch traced here: 231 us
  Pallas kernels  226 us (97%)
  local copies, waits for them, and re-layouts  5.81 us (3%)
    pallas_call x1, Pallas kernels, on_device(): pl.pallas_call(kernel, out_shape=jax.ShapeDtypeStruct((2, 512, 512), F32)...  226 us

profile of v4, /device:TPU:1, one launch (start us, length us, event | category | flops | bytes accessed | tf_op | source)
XLA Modules:
  0.0 231.5 jit_solution(294238596580671367)
XLA Ops:
  0.0 1.3 copy.7.occ_ref
  1.3 1.4 copy.8.vir_ref
  2.7 225.7 %lambda_steps.1 = f32[2,512,512]{2,1,0:T(8,128)} custom-call(f32[2,512,512]{2,1,0:T(8,128)} %bitcast.8, f32[2,8,64,512]{3,2,1,0:T(8,128)} %bitcast.9, f32[8,8,8,1024]{3,2,1,0:T(8,128)} %bitcast.10, s32[1,8192]{1,0:T(1,128)} %bitcast.11, f32[64,1]{1,0:T(8,128)} %copy.7.occ_ref, f32[128,1]{1,0:T(8,128)} %copy.8.vir_ref), custom_call_target="tpu_custom_call" | custom-call | tf_op jit(solution)/shard_map/lambda_steps/pallas_call | solution.py:493
  228.4 3.1 %copy.10 = f32[1024,512]{1,0:T(8,128)} copy(f32[1024,512]{1,0:T(8,128)} %bitcast.7) | data formatting | bytes 4194304

commit v5 on v4

--- a/solution.py
+++ b/solution.py
@@ -62,7 +62,7 @@
     a_ref, v_ref, f_ref, order_ref, occ_ref, vir_ref, o_ref,
     a_in, v_in, f_sib, fk_hl, fr, fr_hl, pa, far_c, near_c, far_r, near_r, mate_c, mate_r,
     sum_c, sum_r, own_c, own_r, inter, y_in, lh, lf, lt, wr, wk,
-    b1, b2, b3, vt_sib, t1, t2, u1, u2, fg, er_ref, ec_ref, ss, rs, ls, fs,
+    b1, b2, b3, vt_sib, t1, t2, u1, u2, fg, er_ref, ec_ref, ss, rs, ls,
 ):
     pb, y_out = f_sib, a_in
     row = lax.axis_index("row")
@@ -243,30 +243,7 @@
     f_copy = send(f_ref, f_sib, sibling)
     f_mine = local(f_ref.at[row], fg.at[k])
     f_mine.wait()
-    moves = []
-
-    def move(i):
-        n = used[0]
-        used[0] += 1
-        far = pltpu.make_async_remote_copy(
-            src_ref=fg.at[i], dst_ref=fr.at[c, row], send_sem=ss.at[n], recv_sem=fs.at[row],
-            device_id=row_ax.device(i), device_id_type=MESH,
-        )
-        near = pltpu.make_async_copy(fg.at[i], fr.at[c, row], fs.at[8])
-        pl.when(i != row)(far.start)
-        pl.when(i == row)(near.start)
-        moves.append((i, far, near))
-
-    def moved():
-        moves[0][2].wait()
-        for j in range(8):
-            come = pltpu.make_async_remote_copy(
-                src_ref=fg.at[j], dst_ref=fr.at[c, j], send_sem=fs.at[9], recv_sem=fs.at[j],
-                device_id=row_ax.device(jnp.int32(j)), device_id_type=MESH,
-            )
-            pl.when(row != j)(come.wait_recv)
-
-    f_gather = Gather(col_ax, fg, move)
+    f_gather = Gather(col_ax, fg)
     f_gather.start()
     v_hop1 = all_to_all(row_ax, lambda i: v_ref.at[:, i], lambda i: b1.at[i])
 
@@ -305,28 +282,33 @@
         rs0[h].start(1)
     f_gather.step3()
     v_copy = send(v_ref.at[o], v_in, sibling)
-    for h in range(2):
-        rs0[h].step(0)
-        rs0[h].step(1)
+    rs0[0].step(0)
+    rs0[0].step(1)
+    rs0[0].to_mate()
+    rs0[1].step(0)
     f_gather.end()
-    for h in range(2):
-        rs0[h].to_mate()
+
+    def start_inter(h):
         chunk(inter, h)[k] = rs0[h].end()
         i_gather[h].start()
-    for h in range(2):
-        i_gather[h].step1()
-        i_gather[h].step2()
+
+    start_inter(0)
+    rs0[1].step(1)
+    rs0[1].to_mate()
+    i_gather[0].step1()
+    i_gather[0].step2()
+    start_inter(1)
+    f_hop = all_to_all(row_ax, lambda i: fg.at[i], lambda i: fr.at[c, i])
     i_gather[0].step3()
-    v_hop1()
+    i_gather[1].step1()
+    i_gather[1].step2()
     i_gather[0].end()
     lf[0, :, :512], lf[1, :, :512] = split(inter[:, :, :, :512].reshape(512, 512))
     i_gather[1].step3()
-    moved()
-    f_copy2 = send(fr.at[c], fr.at[c], sibling)
-    fr_hl[0, c], fr_hl[1, c] = split(fr[c].reshape(512, 1024))
     i_gather[1].end()
+    lf[0, :, 512:], lf[1, :, 512:] = split(inter[:, :, :, 512:].reshape(512, 512))
+    v_hop1()
     v_hop2 = all_to_all(col_ax, lambda i: b1.at[i], lambda i: b2.at[i])
-    lf[0, :, 512:], lf[1, :, 512:] = split(inter[:, :, :, 512:].reshape(512, 512))
 
     v_copy.wait_recv()
 
@@ -359,6 +341,9 @@
         product_nn(lh, fk_hl, pa, h)
         rs1_c[h].start(0)
         rs1_c[h].start(1)
+    f_hop()
+    f_copy2 = send(fr.at[c], fr.at[c], sibling)
+    fr_hl[0, c], fr_hl[1, c] = split(fr[c].reshape(512, 1024))
     y_copy.wait_recv()
 
     @pl.loop(0, 2)
@@ -372,8 +357,9 @@
         product_nn(lt, fr_hl, pb, h)
         rs1_r[h].start(0)
         rs1_r[h].start(1)
-        rs1_c[h].step(0)
-        rs1_c[h].step(1)
+        if h == 0:
+            rs1_c[0].step(0)
+            rs1_c[0].step(1)
 
     c_hop1, r_hop1, c_hop2, r_hop2 = [None] * 2, [None] * 2, [None] * 2, [None] * 2
     k_gather = [Gather(row_ax, chunk(wk, h)) for h in range(2)]
@@ -401,15 +387,17 @@
         col_ax.pick(chunk(wr.at[c], h), k)[...] = own_c[h] + u2[h]
         r_gather[h].start()
 
+    rs1_c[0].to_mate()
+    rs1_c[1].step(0)
     rs1_r[0].step(0)
-    rs1_c[0].to_mate()
     rs1_r[0].step(1)
+    end_c(0)
+    rs1_c[1].step(1)
+    rs1_r[0].to_mate()
+    rs1_r[1].step(0)
     rs1_c[1].to_mate()
-    rs1_r[1].step(0)
+    end_r(0)
     rs1_r[1].step(1)
-    end_c(0)
-    rs1_r[0].to_mate()
-    end_r(0)
     end_c(1)
     rs1_r[1].to_mate()
     v_hop2()
@@ -483,8 +471,6 @@
     vt_copy.wait_recv()
     finish(o, lh, lambda n: vt_sib[pl.ds(n * 4, 4)])
     sent(list(pending.values()))
-    for i, far, _ in moves:
-        pl.when(i != row)(far.wait_send)
 
 
 def on_device(amplitudes, integrals, factors, pair_order, occ_energy, vir_energy):
@@ -534,7 +520,6 @@
             pltpu.SemaphoreType.DMA((N_SEM,)),
             pltpu.SemaphoreType.DMA((N_SEM,)),
             pltpu.SemaphoreType.DMA((16,)),
-            pltpu.SemaphoreType.DMA((10,)),
         ],
         compiler_params=pltpu.CompilerParams(
             collective_id=0, has_side_effects=True, vmem_limit_bytes=63 * 2**20

time: 232 us -> 208 us (0.90)
  Pallas kernels: 226 us -> 201 us
    pallas_call x1, Pallas kernels: 226 us -> 201 us  [on_device(): pl.pallas_call(kernel, out_shape=jax.ShapeDtypeStruct((2, 512, 512), F32)...]
where the time goes in v5:
time: 208 us; the launch traced here: 207 us
  Pallas kernels  201 us (97%)
  local copies, waits for them, and re-layouts  5.81 us (3%)
    pallas_call x1, Pallas kernels, on_device(): pl.pallas_call(kernel, out_shape=jax.ShapeDtypeStruct((2, 512, 512), F32)...  201 us

profile of v5, /device:TPU:1, one launch (start us, length us, event | category | flops | bytes accessed | tf_op | source)
XLA Modules:
  0.0 207.2 jit_solution(16310249191650817517)
XLA Ops:
  0.0 1.3 copy.7.occ_ref
  1.3 1.4 copy.8.vir_ref
  2.7 201.3 %lambda_steps.1 = f32[2,512,512]{2,1,0:T(8,128)} custom-call(f32[2,512,512]{2,1,0:T(8,128)} %bitcast.8, f32[2,8,64,512]{3,2,1,0:T(8,128)} %bitcast.9, f32[8,8,8,1024]{3,2,1,0:T(8,128)} %bitcast.10, s32[1,8192]{1,0:T(1,128)} %bitcast.11, f32[64,1]{1,0:T(8,128)} %copy.7.occ_ref, f32[128,1]{1,0:T(8,128)} %copy.8.vir_ref), custom_call_target="tpu_custom_call" | custom-call | tf_op jit(solution)/shard_map/lambda_steps/pallas_call | solution.py:479
  204.1 3.1 %copy.10 = f32[1024,512]{1,0:T(8,128)} copy(f32[1024,512]{1,0:T(8,128)} %bitcast.7) | data formatting | bytes 4194304

commit v6 on v5

--- a/solution.py
+++ b/solution.py
@@ -144,6 +144,23 @@
 
         return wait
 
+    class Drip:
+        def __init__(self, ax, src, dst):
+            self.ax, self.src, self.dst = ax, src, dst
+            self.mine = local(src(ax.me), dst(ax.me))
+            self.left, self.copies = [4, 3, 5, 2, 6, 1, 7], []
+
+        def __call__(self, n):
+            for d in self.left[:n]:
+                to = rem(self.ax.me + d, 8)
+                self.copies.append(send(self.src(to), self.dst(self.ax.me), self.ax.device(to)))
+            self.left = self.left[n:]
+
+        def wait(self):
+            for copy in self.copies:
+                copy.wait_recv()
+            self.mine.wait()
+
     class Scatter:
         def __init__(self, ax, part, far, near, stage, mate_land):
             self.ax, self.part, self.far, self.near = ax, part, far, near
@@ -298,10 +315,10 @@
     i_gather[0].step1()
     i_gather[0].step2()
     start_inter(1)
-    f_hop = all_to_all(row_ax, lambda i: fg.at[i], lambda i: fr.at[c, i])
     i_gather[0].step3()
     i_gather[1].step1()
     i_gather[1].step2()
+    f_hop = all_to_all(row_ax, lambda i: fg.at[i], lambda i: fr.at[c, i])
     i_gather[0].end()
     lf[0, :, :512], lf[1, :, :512] = split(inter[:, :, :, :512].reshape(512, 512))
     i_gather[1].step3()
@@ -334,6 +351,8 @@
         lh[0, :, at], lh[1, :, at] = split(y)
         lt[0, rows, lanes(c, 512)], lt[1, rows, lanes(c, 512)] = split(y.T)
 
+    f_hop()
+    f_copy2 = send(fr.at[c], fr.at[c], sibling)
     sent(rs0[0].copies() + rs0[1].copies())
     rs1_c = scatters(col_ax, pa, far_c, near_c, sum_c, mate_c)
     rs1_r = scatters(row_ax, pb, far_r, near_r, sum_r, mate_r)
@@ -341,9 +360,6 @@
         product_nn(lh, fk_hl, pa, h)
         rs1_c[h].start(0)
         rs1_c[h].start(1)
-    f_hop()
-    f_copy2 = send(fr.at[c], fr.at[c], sibling)
-    fr_hl[0, c], fr_hl[1, c] = split(fr[c].reshape(512, 1024))
     y_copy.wait_recv()
 
     @pl.loop(0, 2)
@@ -351,6 +367,7 @@
         rows = lanes(n, 256)
         lt[0, rows, lanes(o, 512)], lt[1, rows, lanes(o, 512)] = split(y_in[:, rows].T)
 
+    fr_hl[0, c], fr_hl[1, c] = split(fr[c].reshape(512, 1024))
     f_copy2.wait_recv()
     fr_hl[0, o], fr_hl[1, o] = split(fr[o].reshape(512, 1024))
     for h in range(2):
@@ -400,18 +417,22 @@
     rs1_r[1].step(1)
     end_c(1)
     rs1_r[1].to_mate()
-    v_hop2()
-    v_hop3 = all_to_all(row_ax, lambda i: b2.at[i], lambda i: b3.at[i])
     second_hops(0)
     end_r(1)
     start_gathers(0)
+    v_hop2()
+    v_hop3 = Drip(row_ax, lambda i: b2.at[i], lambda i: b3.at[i])
+    v_hop3(2)
     second_hops(1)
     for gather in (k_gather[0], r_gather[0]):
         gather.step1()
         gather.step2()
     start_gathers(1)
+    v_hop3(1)
+    v_hop3(2)
     k_gather[0].step3()
     r_gather[0].step3()
+    v_hop3(2)
     for gather in (k_gather[1], r_gather[1]):
         gather.step1()
         gather.step2()
@@ -449,7 +470,7 @@
     first(c, lf)
     take_sibling(0, w_copy)
     first(o, lh)
-    v_hop3()
+    v_hop3.wait()
     vt_copy = send(b3.at[:, o], vt_sib, sibling)
     k_gather[1].end()
     r_gather[1].end()

time: 208 us -> 206 us (level)
  no operation moved by 1% of the time
where the time goes in v6:
time: 206 us
  Pallas kernels  200 us (97%)
  local copies, waits for them, and re-layouts  5.81 us (3%)
    pallas_call x1, Pallas kernels, on_device(): pl.pallas_call(kernel, out_shape=jax.ShapeDtypeStruct((2, 512, 512), F32)...  200 us

profile of v6, /device:TPU:1, one launch (start us, length us, event | category | flops | bytes accessed | tf_op | source)
XLA Modules:
  0.0 206.0 jit_solution(1193840108289230756)
XLA Ops:
  0.0 1.3 copy.7.occ_ref
  1.3 1.4 copy.8.vir_ref
  2.7 200.1 %lambda_steps.1 = f32[2,512,512]{2,1,0:T(8,128)} custom-call(f32[2,512,512]{2,1,0:T(8,128)} %bitcast.8, f32[2,8,64,512]{3,2,1,0:T(8,128)} %bitcast.9, f32[8,8,8,1024]{3,2,1,0:T(8,128)} %bitcast.10, s32[1,8192]{1,0:T(1,128)} %bitcast.11, f32[64,1]{1,0:T(8,128)} %copy.7.occ_ref, f32[128,1]{1,0:T(8,128)} %copy.8.vir_ref), custom_call_target="tpu_custom_call" | custom-call | tf_op jit(solution)/shard_map/lambda_steps/pallas_call | solution.py:500
  202.9 3.1 %copy.10 = f32[1024,512]{1,0:T(8,128)} copy(f32[1024,512]{1,0:T(8,128)} %bitcast.7) | data formatting | bytes 4194304

commit v7 on v6

--- a/solution.py
+++ b/solution.py
@@ -16,8 +16,15 @@
 N_SEM = 232
 
 
+def upright(line):
+    n = line.shape[1]
+    here = lax.broadcasted_iota(jnp.int32, (n, n), 0) == lax.broadcasted_iota(jnp.int32, (n, n), 1)
+    return jnp.sum(jnp.where(here, line, 0.0), axis=1, keepdims=True)
+
+
 def pair_energy(codes, occ, vir):
     n = codes.shape[1]
+    occ, vir = upright(occ), upright(vir)
     at_occ = lax.broadcasted_iota(jnp.int32, (NO, n), 0)
     at_vir = lax.broadcasted_iota(jnp.int32, (NV, n), 0)
     occ_hit = at_occ == lax.shift_right_logical(codes, jnp.int32(7))
@@ -551,8 +558,8 @@
         integrals.reshape(2, 8, 64, 512),
         factors.reshape(8, 8, 8, 1024),
         pair_order.reshape(1, NO * NV),
-        occ_energy.reshape(NO, 1),
-        vir_energy.reshape(NV, 1),
+        occ_energy.reshape(1, NO),
+        vir_energy.reshape(1, NV),
     )
     return out.reshape(1024, 512)
 

time: 206 us -> 203 us (0.985)
  local copies, waits for them, and re-layouts: 5.81 us -> 3.08 us
    reshape x2 -> x0, local copies, waits for them, and re-layouts: 2.73 us -> none  [the longest x1 1.39 us: on_device(): vir_energy.reshape(NV, 1)]
where the time goes in v7:
time: 203 us
  Pallas kernels  200 us (99%)
  local copies, waits for them, and re-layouts  3.08 us (2%)
    pallas_call x1, Pallas kernels, on_device(): pl.pallas_call(kernel, out_shape=jax.ShapeDtypeStruct((2, 512, 512), F32)...  200 us

profile of v7, /device:TPU:1, one launch (start us, length us, event | category | flops | bytes accessed | tf_op | source)
XLA Modules:
  0.0 203.2 jit_solution(11088745801700913484)
XLA Ops:
  0.0 200.1 %lambda_steps.1 = f32[2,512,512]{2,1,0:T(8,128)} custom-call(f32[2,512,512]{2,1,0:T(8,128)} %bitcast.8, f32[2,8,64,512]{3,2,1,0:T(8,128)} %bitcast.9, f32[8,8,8,1024]{3,2,1,0:T(8,128)} %bitcast.10, s32[1,8192]{1,0:T(1,128)} %bitcast.11, f32[1,64]{1,0:T(1,128)} %bitcast.12, f32[1,128]{1,0:T(1,128)} %bitcast.13), custom_call_target="tpu_custom_call" | custom-call | tf_op jit(solution)/shard_map/lambda_steps/pallas_call | solution.py:507
  200.1 3.1 %copy.8 = f32[1024,512]{1,0:T(8,128)} copy(f32[1024,512]{1,0:T(8,128)} %bitcast.7) | data formatting | bytes 4194304

commit v8 on v7

--- a/solution.py
+++ b/solution.py
@@ -477,11 +477,11 @@
     first(c, lf)
     take_sibling(0, w_copy)
     first(o, lh)
-    v_hop3.wait()
-    vt_copy = send(b3.at[:, o], vt_sib, sibling)
     k_gather[1].end()
     r_gather[1].end()
     w_copy = take(1)
+    v_hop3.wait()
+    vt_copy = send(b3.at[:, o], vt_sib, sibling)
 
     def finish(half, left, mirrored):
         @pl.loop(0, 2)

time: 203 us -> 203 us (level)
  no operation moved by 1% of the time
where the time goes in v8:
time: 203 us
  Pallas kernels  200 us (99%)
  local copies, waits for them, and re-layouts  3.08 us (2%)
    pallas_call x1, Pallas kernels, on_device(): pl.pallas_call(kernel, out_shape=jax.ShapeDtypeStruct((2, 512, 512), F32)...  200 us

profile of v8, /device:TPU:1, one launch (start us, length us, event | category | flops | bytes accessed | tf_op | source)
XLA Modules:
  0.0 203.0 jit_solution(12456380925070150804)
XLA Ops:
  0.0 199.9 %lambda_steps.1 = f32[2,512,512]{2,1,0:T(8,128)} custom-call(f32[2,512,512]{2,1,0:T(8,128)} %bitcast.8, f32[2,8,64,512]{3,2,1,0:T(8,128)} %bitcast.9, f32[8,8,8,1024]{3,2,1,0:T(8,128)} %bitcast.10, s32[1,8192]{1,0:T(1,128)} %bitcast.11, f32[1,64]{1,0:T(1,128)} %bitcast.12, f32[1,128]{1,0:T(1,128)} %bitcast.13), custom_call_target="tpu_custom_call" | custom-call | tf_op jit(solution)/shard_map/lambda_steps/pallas_call | solution.py:507
  200.0 3.1 %copy.8 = f32[1024,512]{1,0:T(8,128)} copy(f32[1024,512]{1,0:T(8,128)} %bitcast.7) | data formatting | bytes 4194304
